TPU v7x, 32 devices: a whole 2x2x4 slice. The times are simulated.
32 devices in a mesh: groups: 1, dp: 32 (over z, y, x, core).
Axes of the slice: x: 2, y: 2, z: 4, core: 2. Of those that a mesh axis runs over, the one named last changes fastest.
Arguments:
- input_after_norm: bfloat16 [8192, 5120], P(('groups', 'dp')), may hold values from -6 to 6
- value_cotangent: bfloat16 [8192, 1024], P(('groups', 'dp')), may hold values from -6 to 6
- value_weight: bfloat16 [5120, 1024], P('dp'), may hold values from -0.078125 to 0.078125
- down_factors: bfloat16 [5120, 512], P('dp'), may hold values from -0.078125 to 0.078125
- up_factors: bfloat16 [512, 1024], P('dp'), may hold values from -0.1875 to 0.1875
- sequence_adapter: int32 [32], P(('groups', 'dp')), may hold values from 0 to 31
- sequence_loss_length: int32 [32], P(('groups', 'dp')), may hold values from 64 to 256
- adapter_owner_slot: int32 [32], replicated, may hold values from 0 to 31, each once
Outputs:
- input_gradient: bfloat16 [8192, 5120], P(('groups', 'dp'))
- grad_a: float32 [5120, 512], P(('groups', 'dp'))
- grad_b: float32 [512, 1024], P(('groups', 'dp'))
Inputs may be any that keep to these rules, and one draw needn't show every extreme that they name: `sequence_adapter`: every id names an adapter. `adapter_owner_slot`: each adapter has its own slot.
All inputs are finite; a program needn't handle non-finite values.
Results may differ from a plain program's by a relative error of at most 0.0031.
Values may be sent and summed in bfloat16 or wider, within the bound.
No kernel may reach another device: no remote copies, remote signals or barrier semaphores. Data moves between devices by JAX's collectives and lax.ppermute only.
A program may use at most 128 MiB of HBM per device.

v0:
```python
import jax
import jax.numpy as jnp
from jax import lax
from jax.sharding import PartitionSpec as P

ADAPTER_RANK = 16
LENGTH = 256
ADP_DEV = 1


adapter_scale = 2.0


def local(
    input_after_norm,
    value_cotangent,
    value_weight,
    down_factors,
    up_factors,
    sequence_adapter,
    sequence_loss_length,
    adapter_owner_slot,
):
    length = input_after_norm.shape[0]
    width = input_after_norm.shape[1]
    devices = lax.axis_size("dp")
    rows_per_shard = down_factors.shape[0]
    adapter_list = ADP_DEV * devices
    positions = jnp.arange(length)
    value_grad_local = jnp.where(
        (positions < sequence_loss_length[0])[:, None],
        value_cotangent,
        jnp.zeros_like(value_cotangent),
    )
    b_all, ids_all = (
        lax.all_gather(up_factors, "dp", axis=0, tiled=True),
        lax.all_gather(sequence_adapter, "dp", axis=0, tiled=True),
    )
    own_id = sequence_adapter[0]
    own_slot = adapter_owner_slot[own_id]
    up_selected = lax.dynamic_slice_in_dim(b_all, own_slot * ADAPTER_RANK, ADAPTER_RANK, 0)
    down_stacked = down_factors.reshape(rows_per_shard, adapter_list, ADAPTER_RANK)
    sendbuf = jnp.take(down_stacked, ids_all, axis=1)
    down_local = lax.all_to_all(sendbuf, "dp", split_axis=1, concat_axis=0, tiled=True).reshape(
        width, ADAPTER_RANK
    )
    low_rank_gradient = (
        adapter_scale
        * jnp.einsum("dh,ch->dc", value_grad_local, up_selected, preferred_element_type=jnp.float32)
    ).astype(jnp.bfloat16)
    low_rank_update = jnp.dot(
        input_after_norm, down_local, preferred_element_type=jnp.float32
    ).astype(jnp.bfloat16)
    base_term = jnp.einsum(
        "lk,dk->ld",
        value_grad_local,
        lax.all_gather(value_weight, "dp", axis=0, tiled=True),
        preferred_element_type=jnp.float32,
    )
    adapter_term = jnp.einsum(
        "ou,mu->om", low_rank_gradient, down_local, preferred_element_type=jnp.float32
    )
    input_gradient = (base_term + adapter_term).astype(jnp.bfloat16)
    adapter_table = (ids_all[:, None] == jnp.arange(adapter_list)[None, :]).astype(jnp.float32)
    feature_cols = lax.all_to_all(input_after_norm, "dp", split_axis=1, concat_axis=0, tiled=True)
    piece = lax.all_gather(low_rank_gradient, "dp", axis=0, tiled=True)
    count = piece.shape[0] // LENGTH
    input_piece = feature_cols.reshape(count, LENGTH, rows_per_shard)
    gradient_piece = piece.reshape(count, LENGTH, ADAPTER_RANK)
    running_sums = jnp.einsum(
        "ujz,uja->uza", input_piece, gradient_piece, preferred_element_type=jnp.float32
    )
    placed = jnp.einsum("sdr,sa->dar", running_sums, adapter_table, precision=lax.Precision.HIGHEST)
    grad_a = placed.reshape(rows_per_shard, adapter_list * ADAPTER_RANK)
    up_piece = adapter_scale * jnp.einsum(
        "lr,lk->rk", low_rank_update, value_grad_local, preferred_element_type=jnp.float32
    )
    index = jnp.arange(ADP_DEV * ADAPTER_RANK * lax.axis_size("dp"))
    chosen = index // ADAPTER_RANK == own_slot
    values = jnp.take(up_piece, index % ADAPTER_RANK, axis=0)
    grad_b = lax.psum_scatter(
        jnp.where(chosen[:, None], values, jnp.zeros_like(values)),
        "dp",
        scatter_dimension=0,
        tiled=True,
    )
    return (input_gradient, grad_a, grad_b)


def solution(mesh):
    return jax.shard_map(
        local,
        mesh=mesh,
        in_specs=(
            P(("groups", "dp"), None),
            P(("groups", "dp"), None),
            P("dp", None),
            P("dp", None),
            P("dp", None),
            P(("groups", "dp")),
            P(("groups", "dp")),
            P(),
        ),
        out_specs=(P(("groups", "dp"), None), P(("groups", "dp"), None), P(("groups", "dp"), None)),
        check_vma=False,
    )
```

profile of v0, /device:TPU:0, one launch (start us, length us, event | category | flops | bytes accessed | tf_op | source)
XLA Modules:
  0.0 330.6 jit_solution(7885623965057871439)
XLA Ops:
  7.2 0.7 all-gather.5.cloned.1.call-update
  8.0 0.7 all-gather.3.cloned.1.call-update
  9.4 42.0 %all-reduce = s32[32]{0:T(128)S(1)} all-reduce(s32[32]{0:T(128)S(1)} %dynamic-update-slice), channel_id=1, replica_groups=mesh['groups'=1,'dp'=32] {'dp'}, use_global_device_ids=true, to_apply=%add | all-reduce | flops 32 | bytes 256
  51.4 1.0 copy.11
  52.5 0.6 gather_fusion
  53.1 0.8 select_bitcast_fusion
  53.9 4.4 %all-to-all-start = ((bf16[160,32,16]{0,2,1:T(8,128)(2,1)}), bf16[160,32,16]{0,2,1:T(8,128)(2,1)S(1)}, u32[]{:S(2)}, u32[]{:S(2)}) async-start(bf16[160,32,16]{0,2,1:T(8,128)(2,1)} %select_bitcast_fusion), calls=%async_computation | async-start | bytes 524288 | tf_op jit(solution)/shard_map/all_to_all | solution.py:44
  58.3 2.6 copy.13
  60.9 8.8 %all-to-all-done = bf16[160,32,16]{0,2,1:T(8,128)(2,1)S(1)} async-done(((bf16[160,32,16]{0,2,1:T(8,128)(2,1)}), bf16[160,32,16]{0,2,1:T(8,128)(2,1)S(1)}, u32[]{:S(2)}, u32[]{:S(2)}) %all-to-all-start) | async-done | bytes 163872 | tf_op jit(solution)/shard_map/all_to_all | solution.py:44
  69.7 3.7 %all-to-all-start.1 = ((bf16[256,32,160]{0,2,1:T(8,128)(2,1)}), bf16[256,32,160]{0,2,1:T(8,128)(2,1)}, u32[]{:S(2)}, u32[]{:S(2)}) async-start(bf16[256,32,160]{0,2,1:T(8,128)(2,1)} %bitcast.40), calls=%async_computation.1 | async-start | bytes 5242880 | tf_op jit(solution)/shard_map/all_to_all | solution.py:65
  74.1 0.6 dynamic_slice.6
  74.7 0.7 fusion.16
  75.8 2.1 convolution_multiply_fusion
  77.9 1.9 gather_fusion.1
  79.8 1.6 select_select_fusion
  82.1 1.1 fusion.3
  83.2 90.4 %all_gather.15 = bf16[8192,16]{0,1:T(8,128)(2,1)S(1)} all-gather(bf16[256,16]{0,1:T(8,128)(2,1)S(1)} %fusion.3), channel_id=1, replica_groups=mesh['groups'=1,'dp'=32] {'dp'}, dimensions={0}, use_global_device_ids=true | all-gather | bytes 270336 | tf_op jit(solution)/shard_map/all_gather | solution.py:66
  173.6 2.6 fusion.1
  176.1 0.7 convolution_bitcast_fusion
  177.2 0.9 copy.15
  178.1 8.0 %all-gather.3.cloned.1.call-done = bf16[5120,1024]{1,0:T(8,128)(2,1)} async-done(((bf16[160,1024]{1,0:T(8,128)(2,1)}), bf16[5120,1024]{1,0:T(8,128)(2,1)}) %all-gather.3.cloned.1.call-update) | async-done | bytes 10485776 | tf_op jit(solution)/shard_map/all_gather | solution.py:57
  186.1 5.7 %fusion.21 = f32[256,5120]{1,0:T(8,128)S(1)} fusion(bf16[5120,1024]{1,0:T(8,128)(2,1)} %all-gather.3.cloned.1.call-done, bf16[256,1024]{1,0:T(8,128)(2,1)S(1)} %copy-done.1, pred[256]{0:T(512)(128)(4,1)S(1)} %iota_compare_fusion.1), kind=kOutput, calls=%fused_computation.44 | convolution fusion | flops 2684616704 | bytes 16253184 | tf_op jit(solution)/shard_map/lk,dk->ld/dot_general | solution.py:54
  191.7 2.4 fusion
  194.1 130.0 %reduce-scatter.2.cloned.1.call-done = f32[16,1024]{1,0:T(8,128)} async-done(((f32[512,1024]{1,0:T(8,128)}), f32[16,1024]{1,0:T(8,128)}) %reduce-scatter.2.cloned.1.call-update) | async-done | bytes 65552 | tf_op jit(solution)/shard_map/reduce_scatter | solution.py:81
  (23 shorter events, 1.0 us)
Async XLA Ops:
  7.2 51.1 %copy-start = (bf16[256,5120]{1,0:T(8,128)(2,1)S(1)}, bf16[256,5120]{1,0:T(8,128)(2,1)}, u32[]{:S(2)}) copy-start(bf16[256,5120]{1,0:T(8,128)(2,1)} %param.8) | copy-start | bytes 7864324
  7.2 74.9 %all-gather.5.cloned.1.call-start = ((), (), s32[]{:S(2)}) async-start(), calls=%async_computation.4 | async-start | bytes 1081344 | tf_op jit(solution)/shard_map/all_gather | solution.py:36
  7.9 178.2 %all-gather.3.cloned.1.call-start = ((), (), s32[]{:S(2)}) async-start(), calls=%async_computation.3 | async-start | bytes 10813440 | tf_op jit(solution)/shard_map/all_gather | solution.py:57
  53.9 15.8 %all-to-all-start = ((bf16[160,32,16]{0,2,1:T(8,128)(2,1)}), bf16[160,32,16]{0,2,1:T(8,128)(2,1)S(1)}, u32[]{:S(2)}, u32[]{:S(2)}) async-start(bf16[160,32,16]{0,2,1:T(8,128)(2,1)} %select_bitcast_fusion), calls=%async_computation | async-start | bytes 524288 | tf_op jit(solution)/shard_map/all_to_all | solution.py:44
  69.7 4.4 %copy-start.2 = (s32[32]{0:T(128)S(1)}, s32[32]{0:T(128)}, u32[]{:S(2)}) copy-start(s32[32]{0:T(128)} %param.15) | copy-start | bytes 388
  69.7 103.9 %all-to-all-start.1 = ((bf16[256,32,160]{0,2,1:T(8,128)(2,1)}), bf16[256,32,160]{0,2,1:T(8,128)(2,1)}, u32[]{:S(2)}, u32[]{:S(2)}) async-start(bf16[256,32,160]{0,2,1:T(8,128)(2,1)} %bitcast.40), calls=%async_computation.1 | async-start | bytes 5242880 | tf_op jit(solution)/shard_map/all_to_all | solution.py:65
  73.4 250.7 %reduce-scatter.2.cloned.1.call-start = ((), (), s32[]{:S(2)}) async-start(), calls=%async_computation.5 | async-start | bytes 2162688 | tf_op jit(solution)/shard_map/reduce_scatter | solution.py:81
  79.8 2.3 copy-start.1
Sparse Core Ops, SparseCore 0:
  10.9 57.2 all-gather.4
  71.0 114.9 all-gather.2
  188.9 135.1 reduce-scatter.1
where the time goes:
time: 331 us
  waiting for transfers between devices  148 us (45%)
  blocking collectives  132 us (40%)
  between operations  15.9 us (5%)
  matrix products  14.5 us (4%)
  local copies, waits for them, and re-layouts  8.44 us (3%)
  starting transfers between devices  8.18 us (2%)
    reduce_scatter x1, waiting for transfers between devices, local(): lax.psum_scatter(jnp.where(chosen[:, None], values, jnp.zeros_like(values...  130 us
    all_gather x1, blocking collectives, local(): piece = lax.all_gather(low_rank_gradient, 'dp', axis=0, tiled=True)  90.4 us
    unnamed x1, blocking collectives  42 us
    all_to_all x1, waiting for transfers between devices, local(): lax.all_to_all(sendbuf, 'dp', split_axis=1, concat_axis=0, tiled=True)  8.83 us
    all_gather x1, waiting for transfers between devices, local(): lax.all_gather(value_weight, 'dp', axis=0, tiled=True)  7.99 us
  transfers between devices with their start and end apart: 5, of which 3 were waited for; matrix products, arithmetic and copies ran while one was open for 8% of the time, Pallas kernels for 0%

commit v1 on v0

v1 whole, which is shorter than its diff:
```python
import functools

import jax
import jax.numpy as jnp
from jax import lax
from jax.experimental import pallas as pl
from jax.experimental.pallas import tpu as pltpu
from jax.sharding import PartitionSpec as P

RANK = 16
LANES = 128
SCALE = 2.0
BF16 = jnp.bfloat16
F32 = jnp.float32
CONTRACT_LANES = (((1,), (1,)), ((), ()))
CONTRACT_ROWS = (((0,), (0,)), ((), ()))
CONTRACT_INNER = (((1,), (0,)), ((), ()))
VMEM = pl.BlockSpec(memory_space=pltpu.VMEM)
SMEM = pl.BlockSpec(memory_space=pltpu.SMEM)


def dot(a, b, dims):
    return lax.dot_general(a, b, dims, preferred_element_type=F32)


def params(megabytes):
    return pltpu.CompilerParams(vmem_limit_bytes=megabytes << 20)


def selectors(met_ref, slots_ref, id_lane):
    rows = met_ref.shape[0]
    adapter = met_ref[:, id_lane:id_lane + 1].astype(F32).astype(jnp.int32)
    lane = lax.broadcasted_iota(jnp.int32, (rows, slots_ref.shape[1]), 1)
    slot = jnp.sum(jnp.where(lane == adapter, slots_ref[...], 0).astype(F32), axis=1, keepdims=True)
    slot = slot.astype(jnp.int32)
    column = lax.broadcasted_iota(jnp.int32, (rows, rows), 1)
    rank = lax.broadcasted_iota(jnp.int32, (rows, 1), 0) % RANK
    by_adapter = jnp.where(column == adapter * RANK + rank, 1.0, 0.0).astype(BF16)
    by_slot = jnp.where(column == slot * RANK + rank, 1.0, 0.0).astype(BF16)
    return by_adapter, by_slot


def pick_kernel(chunk, met_ref, down_ref, slots_ref, out_ref):
    by_adapter, by_slot = selectors(met_ref, slots_ref, chunk)
    rows = down_ref.shape[0]
    out_ref[:, :rows] = dot(by_adapter, down_ref[...], CONTRACT_LANES).astype(BF16)
    picked = dot(by_slot, met_ref[...], CONTRACT_INNER).astype(BF16)
    out_ref[:, rows:rows + chunk] = picked[:, :chunk]


def place_kernel(chunk, met_ref, slots_ref, sums_ref, down_ref, up_ref):
    by_adapter, by_slot = selectors(met_ref, slots_ref, chunk)
    rows = down_ref.shape[0]
    down_ref[...] = dot(sums_ref[:, :rows], by_adapter, CONTRACT_ROWS)
    up_ref[...] = dot(by_slot, sums_ref[:, rows:rows + chunk], CONTRACT_ROWS)


def masked(dv, length):
    position = lax.broadcasted_iota(jnp.int32, (dv.shape[0], 1), 0)
    return jnp.where(position < length, dv, jnp.zeros_like(dv))


def rank_kernel(rows, chunk, length_ref, x_ref, dv_ref, got_ref, down_ref, g_ref, out_ref, up_ref):
    devices = got_ref.shape[0]
    for j in range(devices):
        down_ref[:, j * rows:(j + 1) * rows] = got_ref[j, :, :rows]
        up_ref[:, j * chunk:(j + 1) * chunk] = got_ref[j, :, rows:rows + chunk]
    dv = masked(dv_ref[...], length_ref[0])
    g = (SCALE * dot(up_ref[...], dv, CONTRACT_LANES)).astype(BF16)
    g_ref[...] = g
    u = dot(down_ref[...], x_ref[...], CONTRACT_LANES).astype(BF16)
    down_sum = dot(g, x_ref[...], CONTRACT_INNER).astype(BF16)
    up_sum = (SCALE * dot(u, dv, CONTRACT_INNER)).astype(BF16)
    for j in range(devices):
        out_ref[j, :, :rows] = down_sum[:, j * rows:(j + 1) * rows]
        out_ref[j, :, rows:rows + chunk] = up_sum[:, j * chunk:(j + 1) * chunk]


def product_kernel(length_ref, dv_ref, g_ref, w_ref, down_ref, out_ref):
    dv = masked(dv_ref[...], length_ref[0])
    base = dot(dv, w_ref[...], CONTRACT_LANES)
    out_ref[...] = (base + dot(g_ref[...], down_ref[...], CONTRACT_ROWS)).astype(BF16)


def local(x, dv, weight, down, up, sequence_adapter, loss_length, owner_slot):
    devices = lax.axis_size("dp")
    tokens, width = x.shape
    value = dv.shape[1]
    rows = down.shape[0]
    chunk = value // devices
    ranks = devices * RANK
    slots = owner_slot.reshape(1, devices)

    weights = lax.all_gather(weight, "dp", axis=0, tiled=True)

    own_up = up.reshape(RANK, devices, chunk).transpose(1, 0, 2)
    own_id = jnp.broadcast_to(sequence_adapter.astype(BF16).reshape(1, 1, 1), (devices, RANK, 1))
    first = jnp.concatenate([own_up, own_id, jnp.zeros((devices, RANK, LANES - 1 - chunk), BF16)], axis=2)
    met = lax.all_to_all(first, "dp", split_axis=0, concat_axis=0, tiled=True).reshape(ranks, LANES)

    second = pl.pallas_call(
        functools.partial(pick_kernel, chunk),
        out_shape=jax.ShapeDtypeStruct((ranks, rows + chunk), BF16),
        in_specs=[VMEM, VMEM, VMEM],
        out_specs=VMEM,
        compiler_params=params(48),
    )(met, down, slots)
    got = lax.all_to_all(second.reshape(devices, RANK, rows + chunk), "dp", split_axis=0, concat_axis=0, tiled=True)

    own_down, g, third = pl.pallas_call(
        functools.partial(rank_kernel, rows, chunk),
        out_shape=(
            jax.ShapeDtypeStruct((RANK, width), BF16),
            jax.ShapeDtypeStruct((RANK, tokens), BF16),
            jax.ShapeDtypeStruct((devices, RANK, rows + chunk), BF16),
        ),
        in_specs=[SMEM, VMEM, VMEM, VMEM],
        out_specs=(VMEM, VMEM, VMEM),
        scratch_shapes=[pltpu.VMEM((RANK, value), BF16)],
        compiler_params=params(48),
    )(loss_length, x, dv, got)
    sums = lax.all_to_all(third, "dp", split_axis=0, concat_axis=0, tiled=True).reshape(ranks, rows + chunk)

    grad_down, slot_sums = pl.pallas_call(
        functools.partial(place_kernel, chunk),
        out_shape=(jax.ShapeDtypeStruct((rows, ranks), F32), jax.ShapeDtypeStruct((ranks, chunk), F32)),
        in_specs=[VMEM, VMEM, VMEM],
        out_specs=(VMEM, VMEM),
        compiler_params=params(48),
    )(met, slots, sums)
    fourth = lax.all_to_all(slot_sums.reshape(devices, RANK, chunk), "dp", split_axis=0, concat_axis=0, tiled=True)
    grad_up = fourth.transpose(1, 0, 2).reshape(RANK, value)

    tile = 640
    grad_x = pl.pallas_call(
        product_kernel,
        out_shape=jax.ShapeDtypeStruct((tokens, width), BF16),
        grid=(width // tile,),
        in_specs=[
            SMEM,
            pl.BlockSpec((tokens, value), lambda i: (0, 0)),
            pl.BlockSpec((RANK, tokens), lambda i: (0, 0)),
            pl.BlockSpec((tile, value), lambda i: (i, 0)),
            pl.BlockSpec((RANK, tile), lambda i: (0, i)),
        ],
        out_specs=pl.BlockSpec((tokens, tile), lambda i: (0, i)),
        compiler_params=params(48),
    )(loss_length, dv, g, weights, own_down)
    return grad_x, grad_down, grad_up


def solution(mesh):
    split = P(("groups", "dp"))
    rows = P(("groups", "dp"), None)
    shard = P("dp", None)
    return jax.shard_map(
        local,
        mesh=mesh,
        in_specs=(rows, rows, shard, shard, shard, split, split, P()),
        out_specs=(rows, rows, rows),
        check_vma=False,
    )
```

time: 331 us -> 125 us (0.38)
  waiting for transfers between devices: 148 us -> 38 us
  blocking collectives: 132 us -> 46.1 us
  Pallas kernels: 0 us -> 15 us
  matrix products: 14.5 us -> 0 us
  starting transfers between devices: 8.18 us -> 2.62 us
    reduce_scatter x1 -> x0, waiting for transfers between devices: 130 us -> none  [local(): lax.psum_scatter(jnp.where(chosen[:, None], values, jnp.zeros_like(values...]
    all_gather x1 -> x0, blocking collectives: 90.4 us -> none  [local(): piece = lax.all_gather(low_rank_gradient, 'dp', axis=0, tiled=True)]
    all_to_all x0 -> x3, blocking collectives: none -> 46.1 us  [the longest x1 18.2 us: local(): lax.all_to_all(third, 'dp', split_axis=0, concat_axis=0, tiled=True)]
    unnamed x1 -> x0, blocking collectives: 42 us -> none
    all_gather x2 -> x1, waiting for transfers between devices: 8.01 us -> 27.6 us  [local(): weights = lax.all_gather(weight, 'dp', axis=0, tiled=True)]
    pallas_call x0 -> x4, Pallas kernels: none -> 15 us  [the longest x1 10.2 us: local(): pl.pallas_call(product_kernel, out_shape=jax.ShapeDtypeStruct((tokens, wi...]
    dot_general x6 -> x0, matrix products: 14.5 us -> none  [the longest x1 5.66 us: local(): jnp.einsum('lk,dk->ld', value_grad_local, lax.all_gather(value_weight, 'd...]
    all_to_all x2 -> x1, starting transfers between devices: 8.06 us -> 2.59 us  [local(): lax.all_to_all(second.reshape(devices, RANK, rows + chunk), 'dp', split_a...]
  transfers between devices with their start and end apart: 5 -> 2, of which waited for: 3 -> 2; matrix products, arithmetic and copies ran while one was open for 8% -> 3% of each run, Pallas kernels for 0% -> 4%
where the time goes in v1:
time: 125 us; the launch traced here: 124 us
  blocking collectives  46.1 us (37%)
  waiting for transfers between devices  38 us (30%)
  between operations  15.4 us (12%)
  Pallas kernels  15 us (12%)
  local copies, waits for them, and re-layouts  6.1 us (5%)
  starting transfers between devices  2.62 us (2%)
    all_gather x1, waiting for transfers between devices, local(): weights = lax.all_gather(weight, 'dp', axis=0, tiled=True)  27.6 us
    all_to_all x1, blocking collectives, local(): lax.all_to_all(third, 'dp', split_axis=0, concat_axis=0, tiled=True)  18.2 us
    all_to_all x1, blocking collectives, local(): lax.all_to_all(first, 'dp', split_axis=0, concat_axis=0, tiled=True)  15.4 us
    all_to_all x1, blocking collectives, local(): lax.all_to_all(slot_sums.reshape(devices, RANK, chunk), 'dp', split_axis=...  12.5 us
    pallas_call x1, Pallas kernels, local(): pl.pallas_call(product_kernel, out_shape=jax.ShapeDtypeStruct((tokens, wi...  10.2 us
    all_to_all x1, waiting for transfers between devices, local(): lax.all_to_all(second.reshape(devices, RANK, rows + chunk), 'dp', split_a...  9.77 us
    unnamed x12, local copies, waits for them, and re-layouts  3.59 us
    all_to_all x1, starting transfers between devices, local(): lax.all_to_all(second.reshape(devices, RANK, rows + chunk), 'dp', split_a...  2.59 us
  transfers between devices with their start and end apart: 2, of which 2 were waited for; matrix products, arithmetic and copies ran while one was open for 3% of the time, Pallas kernels for 4%

profile of v1, /device:TPU:0, one launch (start us, length us, event | category | flops | bytes accessed | tf_op | source)
XLA Modules:
  0.0 124.1 jit_solution(8032296408116617498)
XLA Ops:
  7.2 0.7 all-gather.2.cloned.1.call-update
  7.9 0.9 reshape.31
  8.8 0.1 copy.14
  9.6 0.1 pad.1.clone
  9.6 0.1 pad.2.clone
  9.8 15.4 %all_to_all.20 = bf16[32,16,128]{2,1,0:T(8,128)(2,1)S(1)} all-to-all(bf16[32,16,128]{2,1,0:T(8,128)(2,1)S(1)} %maximum_maximum_fusion), channel_id=1, replica_groups=mesh['groups'=1,'dp'=32] {'dp'}, dimensions={0} | all-to-all | bytes 262144 | tf_op jit(solution)/shard_map/all_to_all | solution.py:99
  25.2 0.9 copy-done.2
  26.1 0.7 copy-done.3
  26.8 1.6 %shard_map.103 = bf16[512,192]{1,0:T(8,128)(2,1)} custom-call(bf16[512,128]{1,0:T(8,128)(2,1)S(1)} %bitcast.10, bf16[160,512]{1,0:T(8,128)(2,1)S(1)} %copy-done.2, s32[1,32]{1,0:T(1,128)S(1)} %bitcast.14), custom_call_target="tpu_custom_call" | custom-call | tf_op jit(solution)/shard_map/pallas_call | solution.py:101
  28.4 2.6 %all-to-all-start.1 = ((bf16[32,16,192]{2,1,0:T(8,128)(2,1)}), bf16[32,16,192]{2,1,0:T(8,128)(2,1)S(1)}, u32[]{:S(2)}, u32[]{:S(2)}) async-start(bf16[32,16,192]{2,1,0:T(8,128)(2,1)} %bitcast.4), calls=%async_computation.1 | async-start | bytes 524288 | tf_op jit(solution)/shard_map/all_to_all | solution.py:108
  31.7 9.8 %all-to-all-done.1.got_ref = bf16[32,16,192]{2,1,0:T(8,128)(2,1)S(1)} async-done(((bf16[32,16,192]{2,1,0:T(8,128)(2,1)}), bf16[32,16,192]{2,1,0:T(8,128)(2,1)S(1)}, u32[]{:S(2)}, u32[]{:S(2)}) %all-to-all-start.1) | async-done | bytes 196640 | tf_op jit(solution)/shard_map/all_to_all | solution.py:108
  41.4 1.7 %copy-done = bf16[256,5120]{1,0:T(8,128)(2,1)S(1)} copy-done((bf16[256,5120]{1,0:T(8,128)(2,1)S(1)}, bf16[256,5120]{1,0:T(8,128)(2,1)}, u32[]{:S(2)}) %copy-start) | copy-done | bytes 2621464
  43.2 1.7 %shard_map.104 = (bf16[16,5120]{1,0:T(8,128)(2,1)S(1)}, bf16[16,256]{1,0:T(8,128)(2,1)S(1)}, bf16[32,16,192]{2,1,0:T(8,128)(2,1)S(1)}) custom-call(s32[1]{0:T(128)S(6)} %copy.16.length_ref, bf16[256,5120]{1,0:T(8,128)(2,1)S(1)} %copy-done, bf16[256,1024]{1,0:T(8,128)(2,1)S(1)} %copy-done.1, bf16[32,16,192]{2,1,0:T(8,128)(2,1)S(1)} %all-to-all-done.1.got_ref), custom_call_target="tpu_custom_call" | custom-call | tf_op jit(solution)/shard_map/pallas_call | solution.py:110
  44.8 18.2 %all_to_all.21 = bf16[32,16,192]{2,1,0:T(8,128)(2,1)S(1)} all-to-all(bf16[32,16,192]{2,1,0:T(8,128)(2,1)S(1)} %get-tuple-element.10), channel_id=1, replica_groups=mesh['groups'=1,'dp'=32] {'dp'}, dimensions={0} | all-to-all | bytes 393216 | tf_op jit(solution)/shard_map/all_to_all | solution.py:122
  63.0 1.5 %shard_map.106 = (f32[160,512]{1,0:T(8,128)}, f32[512,32]{1,0:T(8,128)S(1)}) custom-call(bf16[512,128]{1,0:T(8,128)(2,1)S(1)} %bitcast.11, s32[1,32]{1,0:T(1,128)S(1)} %bitcast.15, bf16[512,192]{1,0:T(8,128)(2,1)S(1)} %bitcast.12), custom_call_target="tpu_custom_call" | custom-call | tf_op jit(solution)/shard_map/pallas_call | solution.py:124
  64.5 0.2 reshape.39
  64.7 12.5 %all_to_all.22 = f32[32,1,512]{2,1,0:T(1,128)S(1)} all-to-all(f32[32,1,512]{2,1,0:T(1,128)S(1)} %reshape.39), channel_id=1, replica_groups=mesh['groups'=1,'dp'=32] {'dp'}, dimensions={0} | all-to-all | bytes 131072 | tf_op jit(solution)/shard_map/all_to_all | solution.py:131
  77.2 0.5 broadcast.5
  77.7 0.8 reduce
  78.5 0.1 reshape.40
  78.6 0.1 copy.12
  78.7 0.8 reshape.37
  79.5 27.6 %all-gather.2.cloned.1.call-done.w_ref = bf16[5120,1024]{1,0:T(8,128)(2,1)} async-done(((bf16[160,1024]{1,0:T(8,128)(2,1)}), bf16[5120,1024]{1,0:T(8,128)(2,1)}) %all-gather.2.cloned.1.call-update) | async-done | bytes 10485776 | tf_op jit(solution)/shard_map/all_gather | solution.py:94
  107.1 10.2 %shard_map.105 = bf16[256,5120]{1,0:T(8,128)(2,1)} custom-call(s32[1]{0:T(128)S(6)} %copy.16.length_ref, bf16[256,1024]{1,0:T(8,128)(2,1)S(1)} %copy-done.1, bf16[16,256]{1,0:T(8,128)(2,1)S(1)} %get-tuple-element.8.g_ref, bf16[5120,1024]{1,0:T(8,128)(2,1)} %all-gather.2.cloned.1.call-done.w_ref, bf16[16,5120]{1,0:T(8,128)(2,1)S(1)} %get-tuple-element.9.down_ref), custom_call_target="tpu_custom_call" | custom-call | tf_op jit(solution)/shard_map/pallas_call | solution.py:135
  (10 shorter events, 0.1 us)
Async XLA Ops:
  7.2 34.3 %copy-start.1 = (bf16[256,1024]{1,0:T(8,128)(2,1)S(1)}, bf16[256,1024]{1,0:T(8,128)(2,1)}, u32[]{:S(2)}) copy-start(bf16[256,1024]{1,0:T(8,128)(2,1)} %dv_ref.3) | copy-start | bytes 1572868
  7.2 99.9 %all-gather.2.cloned.1.call-start = ((), (), s32[]{:S(2)}) async-start(), calls=%async_computation.4 | async-start | bytes 10813440 | tf_op jit(solution)/shard_map/all_gather | solution.py:94
  9.8 53.3 %copy-start.4 = (s32[32]{0:T(128)S(1)}, s32[32]{0:T(128)}, u32[]{:S(2)}) copy-start(s32[32]{0:T(128)} %param.15) | copy-start | bytes 388
  25.2 0.9 copy-start.2
  26.1 0.7 copy-start.3
  28.4 13.0 %all-to-all-start.1 = ((bf16[32,16,192]{2,1,0:T(8,128)(2,1)}), bf16[32,16,192]{2,1,0:T(8,128)(2,1)S(1)}, u32[]{:S(2)}, u32[]{:S(2)}) async-start(bf16[32,16,192]{2,1,0:T(8,128)(2,1)} %bitcast.4), calls=%async_computation.1 | async-start | bytes 524288 | tf_op jit(solution)/shard_map/all_to_all | solution.py:108
  41.4 1.7 %copy-start = (bf16[256,5120]{1,0:T(8,128)(2,1)S(1)}, bf16[256,5120]{1,0:T(8,128)(2,1)}, u32[]{:S(2)}) copy-start(bf16[256,5120]{1,0:T(8,128)(2,1)} %x_ref.1) | copy-start | bytes 7864324
Sparse Core Ops, SparseCore 0:
  10.8 96.1 all-gather.1

commit v2 on v1

--- a/solution.py
+++ b/solution.py
@@ -16,6 +16,7 @@
 CONTRACT_ROWS = (((0,), (0,)), ((), ()))
 CONTRACT_INNER = (((1,), (0,)), ((), ()))
 VMEM = pl.BlockSpec(memory_space=pltpu.VMEM)
+ANY = pl.BlockSpec(memory_space=pl.ANY)
 SMEM = pl.BlockSpec(memory_space=pltpu.SMEM)
 
 
@@ -76,10 +77,14 @@
         out_ref[j, :, rows:rows + chunk] = up_sum[:, j * chunk:(j + 1) * chunk]
 
 
-def product_kernel(length_ref, dv_ref, g_ref, w_ref, down_ref, out_ref):
+def product_kernel(half_ref, length_ref, dv_ref, g_ref, w_ref, down_ref, *refs):
     dv = masked(dv_ref[...], length_ref[0])
     base = dot(dv, w_ref[...], CONTRACT_LANES)
-    out_ref[...] = (base + dot(g_ref[...], down_ref[...], CONTRACT_ROWS)).astype(BF16)
+    refs[-1][...] = (base + dot(g_ref[...], down_ref[...], CONTRACT_ROWS)).astype(BF16)
+
+
+def exchange(value):
+    return lax.all_to_all(value, "dp", split_axis=0, concat_axis=0, tiled=True)
 
 
 def local(x, dv, weight, down, up, sequence_adapter, loss_length, owner_slot):
@@ -91,21 +96,26 @@
     ranks = devices * RANK
     slots = owner_slot.reshape(1, devices)
 
-    weights = lax.all_gather(weight, "dp", axis=0, tiled=True)
+    half = devices // 2
+    my_half = (lax.axis_index("dp") // half).astype(jnp.int32)
+    sides = [list(range(half)), list(range(half, devices))]
+    far_shard = lax.ppermute(weight, "dp", [(i, i ^ half) for i in range(devices)])
+    near_weight = lax.all_gather(weight, "dp", axis=0, tiled=True, axis_index_groups=sides)
+    far_weight = lax.all_gather(far_shard, "dp", axis=0, tiled=True, axis_index_groups=sides)
 
     own_up = up.reshape(RANK, devices, chunk).transpose(1, 0, 2)
     own_id = jnp.broadcast_to(sequence_adapter.astype(BF16).reshape(1, 1, 1), (devices, RANK, 1))
     first = jnp.concatenate([own_up, own_id, jnp.zeros((devices, RANK, LANES - 1 - chunk), BF16)], axis=2)
-    met = lax.all_to_all(first, "dp", split_axis=0, concat_axis=0, tiled=True).reshape(ranks, LANES)
+    met = exchange(first).reshape(ranks, LANES)
 
     second = pl.pallas_call(
         functools.partial(pick_kernel, chunk),
         out_shape=jax.ShapeDtypeStruct((ranks, rows + chunk), BF16),
         in_specs=[VMEM, VMEM, VMEM],
         out_specs=VMEM,
-        compiler_params=params(48),
+        compiler_params=params(8),
     )(met, down, slots)
-    got = lax.all_to_all(second.reshape(devices, RANK, rows + chunk), "dp", split_axis=0, concat_axis=0, tiled=True)
+    got = exchange(second.reshape(devices, RANK, rows + chunk))
 
     own_down, g, third = pl.pallas_call(
         functools.partial(rank_kernel, rows, chunk),
@@ -117,35 +127,47 @@
         in_specs=[SMEM, VMEM, VMEM, VMEM],
         out_specs=(VMEM, VMEM, VMEM),
         scratch_shapes=[pltpu.VMEM((RANK, value), BF16)],
-        compiler_params=params(48),
+        compiler_params=params(8),
     )(loss_length, x, dv, got)
-    sums = lax.all_to_all(third, "dp", split_axis=0, concat_axis=0, tiled=True).reshape(ranks, rows + chunk)
+    sums = exchange(third).reshape(ranks, rows + chunk)
 
     grad_down, slot_sums = pl.pallas_call(
         functools.partial(place_kernel, chunk),
         out_shape=(jax.ShapeDtypeStruct((rows, ranks), F32), jax.ShapeDtypeStruct((ranks, chunk), F32)),
         in_specs=[VMEM, VMEM, VMEM],
         out_specs=(VMEM, VMEM),
-        compiler_params=params(48),
+        compiler_params=params(8),
     )(met, slots, sums)
-    fourth = lax.all_to_all(slot_sums.reshape(devices, RANK, chunk), "dp", split_axis=0, concat_axis=0, tiled=True)
+    fourth = exchange(slot_sums.reshape(devices, RANK, chunk))
     grad_up = fourth.transpose(1, 0, 2).reshape(RANK, value)
 
-    tile = 640
-    grad_x = pl.pallas_call(
-        product_kernel,
-        out_shape=jax.ShapeDtypeStruct((tokens, width), BF16),
-        grid=(width // tile,),
-        in_specs=[
-            SMEM,
-            pl.BlockSpec((tokens, value), lambda i: (0, 0)),
-            pl.BlockSpec((RANK, tokens), lambda i: (0, 0)),
-            pl.BlockSpec((tile, value), lambda i: (i, 0)),
-            pl.BlockSpec((RANK, tile), lambda i: (0, i)),
-        ],
-        out_specs=pl.BlockSpec((tokens, tile), lambda i: (0, i)),
-        compiler_params=params(48),
-    )(loss_length, dv, g, weights, own_down)
+    steps = 2
+    tile = width // (2 * steps)
+
+    def product(half, weights, *earlier):
+        def here(i, half):
+            return 0, half[0] * steps + i
+
+        return pl.pallas_call(
+            product_kernel,
+            out_shape=jax.ShapeDtypeStruct((tokens, width), BF16),
+            grid_spec=pltpu.PrefetchScalarGridSpec(
+                num_scalar_prefetch=1,
+                grid=(steps,),
+                in_specs=[
+                    SMEM,
+                    pl.BlockSpec((tokens, value), lambda i, half: (0, 0)),
+                    pl.BlockSpec((RANK, tokens), lambda i, half: (0, 0)),
+                    pl.BlockSpec((tile, value), lambda i, half: (i, 0)),
+                    pl.BlockSpec((RANK, tile), here),
+                ] + [ANY] * len(earlier),
+                out_specs=pl.BlockSpec((tokens, tile), here),
+            ),
+            input_output_aliases={6: 0} if earlier else {},
+            compiler_params=params(60),
+        )(half.reshape(1), loss_length, dv, g, weights, own_down, *earlier)
+
+    grad_x = product(1 - my_half, far_weight, product(my_half, near_weight))
     return grad_x, grad_down, grad_up
 
 

time: 125 us -> 113 us (0.904)
  blocking collectives: 46.1 us -> 29.5 us
  starting transfers between devices: 2.62 us -> 9.34 us
  waiting for transfers between devices: 38 us -> 35.3 us
  local copies, waits for them, and re-layouts: 6.1 us -> 7.53 us
    all_gather x1 -> x2, waiting for transfers between devices: 27.6 us -> 2.14 us  [the longest x1 2.14 us: local(): lax.all_gather(far_shard, 'dp', axis=0, tiled=True, axis_index_groups=sides)]
    all_to_all x3 -> x2, blocking collectives: 46.1 us -> 29.5 us  [exchange(): return lax.all_to_all(value, 'dp', split_axis=0, concat_axis=0, tiled=True)]
    ppermute x0 -> x1, waiting for transfers between devices: none -> 15.1 us  [local(): lax.ppermute(weight, 'dp', [(i, i ^ half) for i in range(devices)])]
    all_to_all x1 -> x2, waiting for transfers between devices: 9.77 us -> 17.4 us  [exchange(): return lax.all_to_all(value, 'dp', split_axis=0, concat_axis=0, tiled=True)]
    ppermute x0 -> x1, starting transfers between devices: none -> 4.1 us  [local(): lax.ppermute(weight, 'dp', [(i, i ^ half) for i in range(devices)])]
    all_to_all x1 -> x2, starting transfers between devices: 2.59 us -> 5.16 us  [exchange(): return lax.all_to_all(value, 'dp', split_axis=0, concat_axis=0, tiled=True)]
    unnamed x12 -> x18, local copies, waits for them, and re-layouts: 3.59 us -> 5.02 us
    pallas_call x1 -> x2, Pallas kernels: 10.2 us -> 9.69 us  [product(): pl.pallas_call(product_kernel, out_shape=jax.ShapeDtypeStruct((tokens, wi...]
  transfers between devices with their start and end apart: 2 -> 5, of which waited for: 2 -> 4; matrix products, arithmetic and copies ran while one was open for 3% -> 4% of each run, Pallas kernels for 4% -> 9%
where the time goes in v2:
time: 113 us; the launch traced here: 112 us
  waiting for transfers between devices  35.3 us (31%)
  blocking collectives  29.5 us (26%)
  between operations  15.5 us (14%)
  Pallas kernels  14.5 us (13%)
  starting transfers between devices  9.34 us (8%)
  local copies, waits for them, and re-layouts  7.53 us (7%)
    all_to_all x2, blocking collectives, exchange(): return lax.all_to_all(value, 'dp', split_axis=0, concat_axis=0, tiled=True)  29.5 us
    all_to_all x2, waiting for transfers between devices, exchange(): return lax.all_to_all(value, 'dp', split_axis=0, concat_axis=0, tiled=True)  17.4 us
    ppermute x1, waiting for transfers between devices, local(): lax.ppermute(weight, 'dp', [(i, i ^ half) for i in range(devices)])  15.1 us
    pallas_call x2, Pallas kernels, product(): pl.pallas_call(product_kernel, out_shape=jax.ShapeDtypeStruct((tokens, wi...  9.69 us
    all_to_all x2, starting transfers between devices, exchange(): return lax.all_to_all(value, 'dp', split_axis=0, concat_axis=0, tiled=True)  5.16 us
    unnamed x18, local copies, waits for them, and re-layouts  5.02 us
    ppermute x1, starting transfers between devices, local(): lax.ppermute(weight, 'dp', [(i, i ^ half) for i in range(devices)])  4.1 us
  transfers between devices with their start and end apart: 5, of which 4 were waited for; matrix products, arithmetic and copies ran while one was open for 4% of the time, Pallas kernels for 9%

profile of v2, /device:TPU:0, one launch (start us, length us, event | category | flops | bytes accessed | tf_op | source)
XLA Modules:
  0.0 112.5 jit_solution(8424495122598930515)
XLA Ops:
  7.2 0.7 all-gather.5.cloned.1.call-update
  8.0 4.1 %collective-permute-start = (bf16[160,1024]{1,0:T(8,128)(2,1)}, bf16[160,1024]{1,0:T(8,128)(2,1)S(1)}, u32[]{:S(2)}, u32[]{:S(2)}) collective-permute-start(bf16[160,1024]{1,0:T(8,128)(2,1)} %param.10), channel_id=1, source_target_pairs={{0,16},{1,17},{2,18},{3,19},{4,20},{5,21},{6,22},{7,23},{8,24},{9,... | collective-permute-start | bytes 983048 | tf_op jit(solution)/shard_map/ppermute | solution.py:102
  12.1 15.1 %collective-permute-done = bf16[160,1024]{1,0:T(8,128)(2,1)S(1)} collective-permute-done((bf16[160,1024]{1,0:T(8,128)(2,1)}, bf16[160,1024]{1,0:T(8,128)(2,1)S(1)}, u32[]{:S(2)}, u32[]{:S(2)}) %collective-permute-start) | collective-permute-done | bytes 327712 | tf_op jit(solution)/shard_map/ppermute | solution.py:102
  27.1 0.7 copy-done.7
  28.7 0.9 reshape.38
  29.7 14.6 %all_to_all.20 = bf16[32,16,128]{2,1,0:T(8,128)(2,1)S(1)} all-to-all(bf16[32,16,128]{2,1,0:T(8,128)(2,1)S(1)} %maximum_maximum_fusion), channel_id=1, replica_groups=mesh['groups'=1,'dp'=32] {'dp'}, dimensions={0} | all-to-all | bytes 262144 | tf_op jit(solution)/shard_map/all_to_all | solution.py:87
  44.4 0.9 copy-done.3
  45.4 0.7 copy-done.5
  46.0 1.6 %shard_map.103 = bf16[512,192]{1,0:T(8,128)(2,1)} custom-call(bf16[512,128]{1,0:T(8,128)(2,1)S(1)} %bitcast.12, bf16[160,512]{1,0:T(8,128)(2,1)S(1)} %copy-done.3, s32[1,32]{1,0:T(1,128)S(1)} %bitcast.16), custom_call_target="tpu_custom_call" | custom-call | tf_op jit(solution)/shard_map/pallas_call | solution.py:111
  47.6 2.6 %all-to-all-start.1 = ((bf16[32,16,192]{2,1,0:T(8,128)(2,1)}), bf16[32,16,192]{2,1,0:T(8,128)(2,1)S(1)}, u32[]{:S(2)}, u32[]{:S(2)}) async-start(bf16[32,16,192]{2,1,0:T(8,128)(2,1)} %bitcast.5), calls=%async_computation.1 | async-start | bytes 524288 | tf_op jit(solution)/shard_map/all_to_all | solution.py:87
  50.9 9.9 %all-to-all-done.1.got_ref = bf16[32,16,192]{2,1,0:T(8,128)(2,1)S(1)} async-done(((bf16[32,16,192]{2,1,0:T(8,128)(2,1)}), bf16[32,16,192]{2,1,0:T(8,128)(2,1)S(1)}, u32[]{:S(2)}, u32[]{:S(2)}) %all-to-all-start.1) | async-done | bytes 196640 | tf_op jit(solution)/shard_map/all_to_all | solution.py:87
  60.8 1.7 %copy-done.1 = bf16[256,5120]{1,0:T(8,128)(2,1)S(1)} copy-done((bf16[256,5120]{1,0:T(8,128)(2,1)S(1)}, bf16[256,5120]{1,0:T(8,128)(2,1)}, u32[]{:S(2)}) %copy-start.1) | copy-done | bytes 2621464
  62.6 1.7 %shard_map.104 = (bf16[16,5120]{1,0:T(8,128)(2,1)S(1)}, bf16[16,256]{1,0:T(8,128)(2,1)S(1)}, bf16[32,16,192]{2,1,0:T(8,128)(2,1)S(1)}) custom-call(s32[1]{0:T(128)S(6)} %copy.18.length_ref, bf16[256,5120]{1,0:T(8,128)(2,1)S(1)} %copy-done.1, bf16[256,1024]{1,0:T(8,128)(2,1)S(1)} %copy-done, bf16[32,16,192]{2,1,0:T(8,128)(2,1)S(1)} %all-to-all-done.1.got_ref), custom_call_target="tpu_custom_call" | custom-call | tf_op jit(solution)/shard_map/pallas_call | solution.py:120
  64.3 14.9 %all_to_all.21 = bf16[32,16,192]{2,1,0:T(8,128)(2,1)S(1)} all-to-all(bf16[32,16,192]{2,1,0:T(8,128)(2,1)S(1)} %get-tuple-element.10), channel_id=1, replica_groups=mesh['groups'=1,'dp'=32] {'dp'}, dimensions={0} | all-to-all | bytes 393216 | tf_op jit(solution)/shard_map/all_to_all | solution.py:87
  79.2 1.5 %shard_map.107 = (f32[160,512]{1,0:T(8,128)}, f32[512,32]{1,0:T(8,128)S(1)}) custom-call(bf16[512,128]{1,0:T(8,128)(2,1)S(1)} %bitcast.13, s32[1,32]{1,0:T(1,128)S(1)} %bitcast.17, bf16[512,192]{1,0:T(8,128)(2,1)S(1)} %bitcast.14), custom_call_target="tpu_custom_call" | custom-call | tf_op jit(solution)/shard_map/pallas_call | solution.py:134
  80.7 0.8 reshape.47
  81.5 2.6 %all-to-all-start.3 = ((f32[32,1,512]{2,1,0:T(1,128)}), f32[32,1,512]{2,1,0:T(1,128)S(1)}, u32[]{:S(2)}, u32[]{:S(2)}) async-start(f32[32,1,512]{2,1,0:T(1,128)} %reshape.47), calls=%async_computation.3 | async-start | bytes 131072 | tf_op jit(solution)/shard_map/all_to_all | solution.py:87
  84.0 7.4 %all-to-all-done.3 = f32[32,1,512]{2,1,0:T(1,128)S(1)} async-done(((f32[32,1,512]{2,1,0:T(1,128)}), f32[32,1,512]{2,1,0:T(1,128)S(1)}, u32[]{:S(2)}, u32[]{:S(2)}) %all-to-all-start.3) | async-done | bytes 65568 | tf_op jit(solution)/shard_map/all_to_all | solution.py:87
  91.5 0.5 broadcast.6
  92.0 0.8 reduce
  93.0 0.8 reshape.45
  93.8 4.9 %shard_map.105.refs_0_ = bf16[256,5120]{1,0:T(8,128)(2,1)} custom-call(s32[1]{0:T(128)} %bitcast.6.half_ref, s32[1]{0:T(128)S(6)} %copy.18.length_ref, bf16[256,1024]{1,0:T(8,128)(2,1)} %dv_ref.5, bf16[16,256]{1,0:T(8,128)(2,1)} %copy-done.4, bf16[2560,1024]{1,0:T(8,128)(2,1)} %all-gather.5.cloned.1.call-done.w_ref, bf16[16,5120]{1,0:T(8,128)(2,1)} %copy-done.2), custom_call_target="tpu_custom_call" | custom-call | tf_op jit(solution)/shard_map/pallas_call | solution.py:151
  98.7 2.1 %all-gather.3.cloned.1.call-done.w_ref = bf16[2560,1024]{1,0:T(8,128)(2,1)} async-done(((bf16[160,1024]{1,0:T(8,128)(2,1)}), bf16[2560,1024]{1,0:T(8,128)(2,1)}) %all-gather.3.cloned.1.call-update) | async-done | bytes 5242896 | tf_op jit(solution)/shard_map/all_gather | solution.py:104
  100.8 4.8 %shard_map.106 = bf16[256,5120]{1,0:T(8,128)(2,1)} custom-call(s32[1]{0:T(128)} %bitcast.half_ref, s32[1]{0:T(128)S(6)} %copy.18.length_ref, bf16[256,1024]{1,0:T(8,128)(2,1)} %dv_ref.5, bf16[16,256]{1,0:T(8,128)(2,1)} %copy-done.4, bf16[2560,1024]{1,0:T(8,128)(2,1)} %all-gather.3.cloned.1.call-done.w_ref, ...), custom_call_target="tpu_custom_call", output_to_operand_aliasing={{}: (6, {})} | custom-call | tf_op jit(solution)/shard_map/pallas_call | solution.py:151
  (23 shorter events, 0.6 us)
Async XLA Ops:
  7.2 53.7 %copy-start = (bf16[256,1024]{1,0:T(8,128)(2,1)S(1)}, bf16[256,1024]{1,0:T(8,128)(2,1)}, u32[]{:S(2)}) copy-start(bf16[256,1024]{1,0:T(8,128)(2,1)} %dv_ref.5) | copy-start | bytes 1572868
  7.2 86.6 %all-gather.5.cloned.1.call-start = ((), (), s32[]{:S(2)}) async-start(), calls=%async_computation.5 | async-start | bytes 5570560 | tf_op jit(solution)/shard_map/all_gather | solution.py:103
  7.9 92.9 %all-gather.3.cloned.1.call-start = ((), (), s32[]{:S(2)}) async-start(), calls=%async_computation.4 | async-start | bytes 5570560 | tf_op jit(solution)/shard_map/all_gather | solution.py:104
  8.0 19.2 %collective-permute-start = (bf16[160,1024]{1,0:T(8,128)(2,1)}, bf16[160,1024]{1,0:T(8,128)(2,1)S(1)}, u32[]{:S(2)}, u32[]{:S(2)}) collective-permute-start(bf16[160,1024]{1,0:T(8,128)(2,1)} %param.10), channel_id=1, source_target_pairs={{0,16},{1,17},{2,18},{3,19},{4,20},{5,21},{6,22},{7,23},{8,24},{9,... | collective-permute-start | bytes 983048 | tf_op jit(solution)/shard_map/ppermute | solution.py:102
  27.1 0.7 copy-start.7
  29.7 49.4 %copy-start.6 = (s32[32]{0:T(128)S(1)}, s32[32]{0:T(128)}, u32[]{:S(2)}) copy-start(s32[32]{0:T(128)} %param.15) | copy-start | bytes 388
  44.4 0.9 copy-start.3
  45.3 0.7 copy-start.5
  47.6 13.2 %all-to-all-start.1 = ((bf16[32,16,192]{2,1,0:T(8,128)(2,1)}), bf16[32,16,192]{2,1,0:T(8,128)(2,1)S(1)}, u32[]{:S(2)}, u32[]{:S(2)}) async-start(bf16[32,16,192]{2,1,0:T(8,128)(2,1)} %bitcast.5), calls=%async_computation.1 | async-start | bytes 524288 | tf_op jit(solution)/shard_map/all_to_all | solution.py:87
  60.8 1.7 %copy-start.1 = (bf16[256,5120]{1,0:T(8,128)(2,1)S(1)}, bf16[256,5120]{1,0:T(8,128)(2,1)}, u32[]{:S(2)}) copy-start(bf16[256,5120]{1,0:T(8,128)(2,1)} %x_ref.1) | copy-start | bytes 7864324
  64.3 16.4 %copy-start.2 = (bf16[16,5120]{1,0:T(8,128)(2,1)}, bf16[16,5120]{1,0:T(8,128)(2,1)S(1)}, u32[]{:S(2)}) copy-start(bf16[16,5120]{1,0:T(8,128)(2,1)S(1)} %get-tuple-element.9.down_ref) | copy-start | bytes 491524
  64.3 16.4 %copy-start.4 = (bf16[16,256]{1,0:T(8,128)(2,1)}, bf16[16,256]{1,0:T(8,128)(2,1)S(1)}, u32[]{:S(2)}) copy-start(bf16[16,256]{1,0:T(8,128)(2,1)S(1)} %get-tuple-element.8.g_ref) | copy-start | bytes 24580
  81.5 10.0 %all-to-all-start.3 = ((f32[32,1,512]{2,1,0:T(1,128)}), f32[32,1,512]{2,1,0:T(1,128)S(1)}, u32[]{:S(2)}, u32[]{:S(2)}) async-start(f32[32,1,512]{2,1,0:T(1,128)} %reshape.47), calls=%async_computation.3 | async-start | bytes 131072 | tf_op jit(solution)/shard_map/all_to_all | solution.py:87
Sparse Core Ops, SparseCore 0:
  9.6 46.1 all-gather.4
  57.4 43.3 all-gather.2

commit v3 on v1

--- a/solution.py
+++ b/solution.py
@@ -16,6 +16,7 @@
 CONTRACT_ROWS = (((0,), (0,)), ((), ()))
 CONTRACT_INNER = (((1,), (0,)), ((), ()))
 VMEM = pl.BlockSpec(memory_space=pltpu.VMEM)
+HBM = pl.BlockSpec(memory_space=pltpu.HBM)
 SMEM = pl.BlockSpec(memory_space=pltpu.SMEM)
 
 
@@ -76,10 +77,43 @@
         out_ref[j, :, rows:rows + chunk] = up_sum[:, j * chunk:(j + 1) * chunk]
 
 
-def product_kernel(length_ref, dv_ref, g_ref, w_ref, down_ref, out_ref):
+def product_kernel(order, length_ref, dv_ref, g_ref, down_ref, w_ref, out_ref, held_ref, block_ref, sem, out_sem):
+    groups, places, rows, _ = held_ref.shape
+    copies = [[] for _ in range(groups)]
+    for position, block in enumerate(order):
+        source = w_ref.at[pl.ds(position * rows, rows)]
+        group, place = block // places, block % places
+        copies[group].append(pltpu.make_async_copy(source, held_ref.at[group, place], sem.at[group, place]))
+
+    def leave(group):
+        target = out_ref.at[:, pl.ds(group * places * rows, places * rows)]
+        return pltpu.make_async_copy(block_ref.at[group], target, out_sem.at[group])
+
+    for group in copies:
+        for copy in group:
+            copy.start()
     dv = masked(dv_ref[...], length_ref[0])
-    base = dot(dv, w_ref[...], CONTRACT_LANES)
-    out_ref[...] = (base + dot(g_ref[...], down_ref[...], CONTRACT_ROWS)).astype(BF16)
+    for group in range(groups):
+        for copy in copies[group]:
+            copy.wait()
+        weight = held_ref[group].reshape(places * rows, dv.shape[1])
+        columns = slice(group * places * rows, (group + 1) * places * rows)
+        total = dot(dv, weight, CONTRACT_LANES) + dot(g_ref[...], down_ref[:, columns], CONTRACT_ROWS)
+        block_ref[group] = total.astype(BF16)
+        leave(group).start()
+    for group in range(groups):
+        leave(group).wait()
+
+
+def snake(sizes):
+    path = [0]
+    for size in sizes:
+        path = [i * size + k for at, i in enumerate(path) for k in (range(size) if at % 2 == 0 else reversed(range(size)))]
+    return path
+
+
+def exchange(value):
+    return lax.all_to_all(value, "dp", split_axis=0, concat_axis=0, tiled=True)
 
 
 def local(x, dv, weight, down, up, sequence_adapter, loss_length, owner_slot):
@@ -91,21 +125,25 @@
     ranks = devices * RANK
     slots = owner_slot.reshape(1, devices)
 
-    weights = lax.all_gather(weight, "dp", axis=0, tiled=True)
+    chips = devices // 2
+    side = int(chips ** 0.5)
+    path = snake((chips // 4, 2, 2) if chips <= 16 else (side, chips // side))
+    ring = [2 * chip + core for chip in path for core in range(2)]
+    weights = lax.all_gather(weight, "dp", axis=0, tiled=True, axis_index_groups=[ring])
 
     own_up = up.reshape(RANK, devices, chunk).transpose(1, 0, 2)
     own_id = jnp.broadcast_to(sequence_adapter.astype(BF16).reshape(1, 1, 1), (devices, RANK, 1))
     first = jnp.concatenate([own_up, own_id, jnp.zeros((devices, RANK, LANES - 1 - chunk), BF16)], axis=2)
-    met = lax.all_to_all(first, "dp", split_axis=0, concat_axis=0, tiled=True).reshape(ranks, LANES)
+    met = exchange(first).reshape(ranks, LANES)
 
     second = pl.pallas_call(
         functools.partial(pick_kernel, chunk),
         out_shape=jax.ShapeDtypeStruct((ranks, rows + chunk), BF16),
         in_specs=[VMEM, VMEM, VMEM],
         out_specs=VMEM,
-        compiler_params=params(48),
+        compiler_params=params(8),
     )(met, down, slots)
-    got = lax.all_to_all(second.reshape(devices, RANK, rows + chunk), "dp", split_axis=0, concat_axis=0, tiled=True)
+    got = exchange(second.reshape(devices, RANK, rows + chunk))
 
     own_down, g, third = pl.pallas_call(
         functools.partial(rank_kernel, rows, chunk),
@@ -117,35 +155,41 @@
         in_specs=[SMEM, VMEM, VMEM, VMEM],
         out_specs=(VMEM, VMEM, VMEM),
         scratch_shapes=[pltpu.VMEM((RANK, value), BF16)],
-        compiler_params=params(48),
+        compiler_params=params(8),
     )(loss_length, x, dv, got)
-    sums = lax.all_to_all(third, "dp", split_axis=0, concat_axis=0, tiled=True).reshape(ranks, rows + chunk)
+    sums = exchange(third).reshape(ranks, rows + chunk)
 
     grad_down, slot_sums = pl.pallas_call(
         functools.partial(place_kernel, chunk),
         out_shape=(jax.ShapeDtypeStruct((rows, ranks), F32), jax.ShapeDtypeStruct((ranks, chunk), F32)),
         in_specs=[VMEM, VMEM, VMEM],
         out_specs=(VMEM, VMEM),
-        compiler_params=params(48),
+        compiler_params=params(8),
     )(met, slots, sums)
-    fourth = lax.all_to_all(slot_sums.reshape(devices, RANK, chunk), "dp", split_axis=0, concat_axis=0, tiled=True)
+    fourth = exchange(slot_sums.reshape(devices, RANK, chunk))
     grad_up = fourth.transpose(1, 0, 2).reshape(RANK, value)
 
-    tile = 640
+    order, block = path, 2 * rows
+    if block % 16:
+        back = sorted(range(chips), key=lambda position: path[position])
+        weights = weights.reshape(chips, block, value)[jnp.array(back)].reshape(width, value)
+    groups = 4
+    if block % 16 or chips % groups:
+        order, block = list(range(groups)), width // groups
+    places = len(order) // groups
     grad_x = pl.pallas_call(
-        product_kernel,
+        functools.partial(product_kernel, order),
         out_shape=jax.ShapeDtypeStruct((tokens, width), BF16),
-        grid=(width // tile,),
-        in_specs=[
-            SMEM,
-            pl.BlockSpec((tokens, value), lambda i: (0, 0)),
-            pl.BlockSpec((RANK, tokens), lambda i: (0, 0)),
-            pl.BlockSpec((tile, value), lambda i: (i, 0)),
-            pl.BlockSpec((RANK, tile), lambda i: (0, i)),
+        in_specs=[SMEM, VMEM, VMEM, VMEM, HBM],
+        out_specs=HBM,
+        scratch_shapes=[
+            pltpu.VMEM((groups, places, block, value), BF16),
+            pltpu.VMEM((groups, tokens, places * block), BF16),
+            pltpu.SemaphoreType.DMA((groups, places)),
+            pltpu.SemaphoreType.DMA((groups,)),
         ],
-        out_specs=pl.BlockSpec((tokens, tile), lambda i: (0, i)),
-        compiler_params=params(48),
-    )(loss_length, dv, g, weights, own_down)
+        compiler_params=params(60),
+    )(loss_length, dv, g, own_down, weights)
     return grad_x, grad_down, grad_up
 
 

time: 125 us -> 109 us (0.87)
  waiting for transfers between devices: 38 us -> 28.2 us
  blocking collectives: 46.1 us -> 39.3 us
    all_gather x1, waiting for transfers between devices: 27.6 us -> 14.7 us  [local(): lax.all_gather(weight, 'dp', axis=0, tiled=True, axis_index_groups=[ring])]
    all_to_all x3, blocking collectives: 46.1 us -> 39.3 us  [exchange(): return lax.all_to_all(value, 'dp', split_axis=0, concat_axis=0, tiled=True)]
    all_to_all x1, waiting for transfers between devices: 9.77 us -> 12.9 us  [exchange(): return lax.all_to_all(value, 'dp', split_axis=0, concat_axis=0, tiled=True)]
    unnamed x12 -> x16, local copies, waits for them, and re-layouts: 3.59 us -> 3.66 us
where the time goes in v3:
time: 109 us
  blocking collectives  39.3 us (36%)
  waiting for transfers between devices  28.2 us (26%)
  Pallas kernels  16 us (15%)
  between operations  15.5 us (14%)
  local copies, waits for them, and re-layouts  6.16 us (6%)
  starting transfers between devices  2.68 us (2%)
    all_to_all x3, blocking collectives, exchange(): return lax.all_to_all(value, 'dp', split_axis=0, concat_axis=0, tiled=True)  39.3 us
    all_gather x1, waiting for transfers between devices, local(): lax.all_gather(weight, 'dp', axis=0, tiled=True, axis_index_groups=[ring])  14.7 us
    all_to_all x1, waiting for transfers between devices, exchange(): return lax.all_to_all(value, 'dp', split_axis=0, concat_axis=0, tiled=True)  12.9 us
    pallas_call x1, Pallas kernels, local(): pl.pallas_call(functools.partial(product_kernel, order), out_shape=jax.Sh...  11.2 us
    unnamed x16, local copies, waits for them, and re-layouts  3.66 us
    all_to_all x1, starting transfers between devices, exchange(): return lax.all_to_all(value, 'dp', split_axis=0, concat_axis=0, tiled=True)  2.64 us
  transfers between devices with their start and end apart: 2, of which 2 were waited for; matrix products, arithmetic and copies ran while one was open for 3% of the time, Pallas kernels for 4%

profile of v3, /device:TPU:0, one launch (start us, length us, event | category | flops | bytes accessed | tf_op | source)
XLA Modules:
  0.0 108.7 jit_solution(9063978185715440986)
XLA Ops:
  7.2 0.7 all-gather.2.cloned.1.call-update
  7.9 0.9 reshape.31
  8.8 0.1 copy.14
  9.6 0.1 pad.1.clone
  9.6 0.1 pad.2.clone
  9.8 15.3 %all_to_all.20 = bf16[32,16,128]{2,1,0:T(8,128)(2,1)S(1)} all-to-all(bf16[32,16,128]{2,1,0:T(8,128)(2,1)S(1)} %maximum_maximum_fusion), channel_id=1, replica_groups=mesh['groups'=1,'dp'=32] {'dp'}, dimensions={0} | all-to-all | bytes 262144 | tf_op jit(solution)/shard_map/all_to_all | solution.py:116
  25.1 0.9 copy-done.2
  26.0 0.7 copy-done.5
  26.7 1.6 %shard_map.103 = bf16[512,192]{1,0:T(8,128)(2,1)} custom-call(bf16[512,128]{1,0:T(8,128)(2,1)S(1)} %bitcast.10, bf16[160,512]{1,0:T(8,128)(2,1)S(1)} %copy-done.2, s32[1,32]{1,0:T(1,128)S(1)} %bitcast.14), custom_call_target="tpu_custom_call" | custom-call | tf_op jit(solution)/shard_map/pallas_call | solution.py:139
  28.3 2.6 %all-to-all-start.1 = ((bf16[32,16,192]{2,1,0:T(8,128)(2,1)}), bf16[32,16,192]{2,1,0:T(8,128)(2,1)S(1)}, u32[]{:S(2)}, u32[]{:S(2)}) async-start(bf16[32,16,192]{2,1,0:T(8,128)(2,1)} %bitcast.4), calls=%async_computation.1 | async-start | bytes 524288 | tf_op jit(solution)/shard_map/all_to_all | solution.py:116
  31.6 12.9 %all-to-all-done.1.got_ref = bf16[32,16,192]{2,1,0:T(8,128)(2,1)S(1)} async-done(((bf16[32,16,192]{2,1,0:T(8,128)(2,1)}), bf16[32,16,192]{2,1,0:T(8,128)(2,1)S(1)}, u32[]{:S(2)}, u32[]{:S(2)}) %all-to-all-start.1) | async-done | bytes 196640 | tf_op jit(solution)/shard_map/all_to_all | solution.py:116
  44.5 1.8 %copy-done = bf16[256,5120]{1,0:T(8,128)(2,1)S(1)} copy-done((bf16[256,5120]{1,0:T(8,128)(2,1)S(1)}, bf16[256,5120]{1,0:T(8,128)(2,1)}, u32[]{:S(2)}) %copy-start) | copy-done | bytes 2621464
  46.3 1.7 %shard_map.104 = (bf16[16,5120]{1,0:T(8,128)(2,1)S(1)}, bf16[16,256]{1,0:T(8,128)(2,1)S(1)}, bf16[32,16,192]{2,1,0:T(8,128)(2,1)S(1)}) custom-call(s32[1]{0:T(128)S(6)} %copy.16.length_ref, bf16[256,5120]{1,0:T(8,128)(2,1)S(1)} %copy-done, bf16[256,1024]{1,0:T(8,128)(2,1)S(1)} %copy-done.1, bf16[32,16,192]{2,1,0:T(8,128)(2,1)S(1)} %all-to-all-done.1.got_ref), custom_call_target="tpu_custom_call" | custom-call | tf_op jit(solution)/shard_map/pallas_call | solution.py:148
  48.0 14.7 %all_to_all.21 = bf16[32,16,192]{2,1,0:T(8,128)(2,1)S(1)} all-to-all(bf16[32,16,192]{2,1,0:T(8,128)(2,1)S(1)} %get-tuple-element.10), channel_id=1, replica_groups=mesh['groups'=1,'dp'=32] {'dp'}, dimensions={0} | all-to-all | bytes 393216 | tf_op jit(solution)/shard_map/all_to_all | solution.py:116
  62.6 1.5 %shard_map.106 = (f32[160,512]{1,0:T(8,128)}, f32[512,32]{1,0:T(8,128)S(1)}) custom-call(bf16[512,128]{1,0:T(8,128)(2,1)S(1)} %bitcast.11, s32[1,32]{1,0:T(1,128)S(1)} %bitcast.15, bf16[512,192]{1,0:T(8,128)(2,1)S(1)} %bitcast.12), custom_call_target="tpu_custom_call" | custom-call | tf_op jit(solution)/shard_map/pallas_call | solution.py:162
  64.1 0.2 reshape.39
  64.3 9.3 %all_to_all.22 = f32[32,1,512]{2,1,0:T(1,128)S(1)} all-to-all(f32[32,1,512]{2,1,0:T(1,128)S(1)} %reshape.39), channel_id=1, replica_groups=mesh['groups'=1,'dp'=32] {'dp'}, dimensions={0} | all-to-all | bytes 131072 | tf_op jit(solution)/shard_map/all_to_all | solution.py:116
  73.6 0.5 broadcast.5
  74.1 0.8 reduce
  74.9 0.1 reshape.40
  75.0 0.1 copy.12
  75.1 0.8 reshape.37
  75.9 14.7 %all-gather.2.cloned.1.call-done.w_ref = bf16[5120,1024]{1,0:T(8,128)(2,1)} async-done(((bf16[160,1024]{1,0:T(8,128)(2,1)}), bf16[5120,1024]{1,0:T(8,128)(2,1)}) %all-gather.2.cloned.1.call-update) | async-done | bytes 10485776 | tf_op jit(solution)/shard_map/all_gather | solution.py:132
  90.6 11.2 %shard_map.105 = bf16[256,5120]{1,0:T(8,128)(2,1)} custom-call(s32[1]{0:T(128)S(6)} %copy.16.length_ref, bf16[256,1024]{1,0:T(8,128)(2,1)} %dv_ref.3, bf16[16,256]{1,0:T(8,128)(2,1)} %copy-done.4, bf16[16,5120]{1,0:T(8,128)(2,1)} %copy-done.3, bf16[5120,1024]{1,0:T(8,128)(2,1)} %all-gather.2.cloned.1.call-done.w_ref), custom_call_target="tpu_custom_call" | custom-call | tf_op jit(solution)/shard_map/pallas_call | solution.py:180
  (14 shorter events, 0.1 us)
Async XLA Ops:
  7.2 37.3 %copy-start.1 = (bf16[256,1024]{1,0:T(8,128)(2,1)S(1)}, bf16[256,1024]{1,0:T(8,128)(2,1)}, u32[]{:S(2)}) copy-start(bf16[256,1024]{1,0:T(8,128)(2,1)} %dv_ref.3) | copy-start | bytes 1572868
  7.2 83.4 %all-gather.2.cloned.1.call-start = ((), (), s32[]{:S(2)}) async-start(), calls=%async_computation.4 | async-start | bytes 10813440 | tf_op jit(solution)/shard_map/all_gather | solution.py:132
  9.8 52.9 %copy-start.6 = (s32[32]{0:T(128)S(1)}, s32[32]{0:T(128)}, u32[]{:S(2)}) copy-start(s32[32]{0:T(128)} %param.15) | copy-start | bytes 388
  25.1 0.9 copy-start.2
  26.0 0.7 copy-start.5
  28.3 16.2 %all-to-all-start.1 = ((bf16[32,16,192]{2,1,0:T(8,128)(2,1)}), bf16[32,16,192]{2,1,0:T(8,128)(2,1)S(1)}, u32[]{:S(2)}, u32[]{:S(2)}) async-start(bf16[32,16,192]{2,1,0:T(8,128)(2,1)} %bitcast.4), calls=%async_computation.1 | async-start | bytes 524288 | tf_op jit(solution)/shard_map/all_to_all | solution.py:116
  44.5 1.8 %copy-start = (bf16[256,5120]{1,0:T(8,128)(2,1)S(1)}, bf16[256,5120]{1,0:T(8,128)(2,1)}, u32[]{:S(2)}) copy-start(bf16[256,5120]{1,0:T(8,128)(2,1)} %x_ref.1) | copy-start | bytes 7864324
  47.9 16.2 %copy-start.3 = (bf16[16,5120]{1,0:T(8,128)(2,1)}, bf16[16,5120]{1,0:T(8,128)(2,1)S(1)}, u32[]{:S(2)}) copy-start(bf16[16,5120]{1,0:T(8,128)(2,1)S(1)} %get-tuple-element.9.down_ref) | copy-start | bytes 491524
  48.0 16.2 %copy-start.4 = (bf16[16,256]{1,0:T(8,128)(2,1)}, bf16[16,256]{1,0:T(8,128)(2,1)S(1)}, u32[]{:S(2)}) copy-start(bf16[16,256]{1,0:T(8,128)(2,1)S(1)} %get-tuple-element.8.g_ref) | copy-start | bytes 24580
Sparse Core Ops, SparseCore 0:
  9.6 80.9 all-gather.1

commit v4 on v3

--- a/solution.py
+++ b/solution.py
@@ -9,6 +9,7 @@
 
 RANK = 16
 LANES = 128
+COLUMNS = 256
 SCALE = 2.0
 BF16 = jnp.bfloat16
 F32 = jnp.float32
@@ -78,12 +79,13 @@
 
 
 def product_kernel(order, length_ref, dv_ref, g_ref, down_ref, w_ref, out_ref, held_ref, block_ref, sem, out_sem):
-    groups, places, rows, _ = held_ref.shape
+    groups, places = sem.shape
+    rows = held_ref.shape[1] // places
     copies = [[] for _ in range(groups)]
     for position, block in enumerate(order):
         source = w_ref.at[pl.ds(position * rows, rows)]
         group, place = block // places, block % places
-        copies[group].append(pltpu.make_async_copy(source, held_ref.at[group, place], sem.at[group, place]))
+        copies[group].append(pltpu.make_async_copy(source, held_ref.at[group, pl.ds(place * rows, rows)], sem.at[group, place]))
 
     def leave(group):
         target = out_ref.at[:, pl.ds(group * places * rows, places * rows)]
@@ -93,13 +95,15 @@
         for copy in group:
             copy.start()
     dv = masked(dv_ref[...], length_ref[0])
+    g = g_ref[...]
     for group in range(groups):
         for copy in copies[group]:
             copy.wait()
-        weight = held_ref[group].reshape(places * rows, dv.shape[1])
-        columns = slice(group * places * rows, (group + 1) * places * rows)
-        total = dot(dv, weight, CONTRACT_LANES) + dot(g_ref[...], down_ref[:, columns], CONTRACT_ROWS)
-        block_ref[group] = total.astype(BF16)
+        for first in range(0, places * rows, COLUMNS):
+            columns = slice(group * places * rows + first, group * places * rows + first + COLUMNS)
+            total = dot(dv, held_ref[group, first:first + COLUMNS], CONTRACT_LANES)
+            total += dot(g, down_ref[:, columns], CONTRACT_ROWS)
+            block_ref[group, :, first:first + COLUMNS] = total.astype(BF16)
         leave(group).start()
     for group in range(groups):
         leave(group).wait()
@@ -132,9 +136,12 @@
     weights = lax.all_gather(weight, "dp", axis=0, tiled=True, axis_index_groups=[ring])
 
     own_up = up.reshape(RANK, devices, chunk).transpose(1, 0, 2)
-    own_id = jnp.broadcast_to(sequence_adapter.astype(BF16).reshape(1, 1, 1), (devices, RANK, 1))
-    first = jnp.concatenate([own_up, own_id, jnp.zeros((devices, RANK, LANES - 1 - chunk), BF16)], axis=2)
-    met = exchange(first).reshape(ranks, LANES)
+    own_id = jnp.broadcast_to(sequence_adapter.astype(BF16).reshape(1, 1, 1), (devices, 1, LANES))
+    packed = jnp.concatenate([own_up.reshape(devices, -1, LANES), own_id], axis=1)
+    met = exchange(packed)
+    met_up = met[:, :-1].reshape(devices, RANK, chunk)
+    met_id = jnp.broadcast_to(met[:, -1:, :LANES - chunk], (devices, RANK, LANES - chunk))
+    met = jnp.concatenate([met_up, met_id], axis=2).reshape(ranks, LANES)
 
     second = pl.pallas_call(
         functools.partial(pick_kernel, chunk),
@@ -143,7 +150,7 @@
         out_specs=VMEM,
         compiler_params=params(8),
     )(met, down, slots)
-    got = exchange(second.reshape(devices, RANK, rows + chunk))
+    got = exchange(second.reshape(devices, -1, LANES)).reshape(devices, RANK, rows + chunk)
 
     own_down, g, third = pl.pallas_call(
         functools.partial(rank_kernel, rows, chunk),
@@ -157,7 +164,7 @@
         scratch_shapes=[pltpu.VMEM((RANK, value), BF16)],
         compiler_params=params(8),
     )(loss_length, x, dv, got)
-    sums = exchange(third).reshape(ranks, rows + chunk)
+    sums = exchange(third.reshape(devices, -1, LANES)).reshape(ranks, rows + chunk)
 
     grad_down, slot_sums = pl.pallas_call(
         functools.partial(place_kernel, chunk),
@@ -183,7 +190,7 @@
         in_specs=[SMEM, VMEM, VMEM, VMEM, HBM],
         out_specs=HBM,
         scratch_shapes=[
-            pltpu.VMEM((groups, places, block, value), BF16),
+            pltpu.VMEM((groups, places * block, value), BF16),
             pltpu.VMEM((groups, tokens, places * block), BF16),
             pltpu.SemaphoreType.DMA((groups, places)),
             pltpu.SemaphoreType.DMA((groups,)),

time: 109 us -> 103 us (0.945)
  waiting for transfers between devices: 28.2 us -> 23.6 us
  local copies, waits for them, and re-layouts: 6.16 us -> 10.3 us
  Pallas kernels: 16 us -> 12.6 us
  blocking collectives: 39.3 us -> 36.8 us
    reshape x0 -> x5, local copies, waits for them, and re-layouts: none -> 3.73 us  [the longest x1 1.28 us: local(): third.reshape(devices, -1, LANES)]
    pallas_call x1, Pallas kernels: 11.2 us -> 8.48 us  [local(): pl.pallas_call(functools.partial(product_kernel, order), out_shape=jax.Sh...]
    all_gather x1, waiting for transfers between devices: 14.7 us -> 12.1 us  [local(): lax.all_gather(weight, 'dp', axis=0, tiled=True, axis_index_groups=[ring])]
    all_to_all x3, blocking collectives: 39.3 us -> 36.8 us  [exchange(): return lax.all_to_all(value, 'dp', split_axis=0, concat_axis=0, tiled=True)]
    all_to_all x1, waiting for transfers between devices: 12.9 us -> 10.8 us  [exchange(): return lax.all_to_all(value, 'dp', split_axis=0, concat_axis=0, tiled=True)]
    unnamed x16 -> x19, local copies, waits for them, and re-layouts: 3.66 us -> 3.85 us
  transfers between devices with their start and end apart: 2 -> 2, of which waited for: 2 -> 2; matrix products, arithmetic and copies ran while one was open for 3% -> 7% of each run, Pallas kernels for 4% -> 4%
where the time goes in v4:
time: 103 us
  blocking collectives  36.8 us (36%)
  waiting for transfers between devices  23.6 us (23%)
  between operations  15.6 us (15%)
  Pallas kernels  12.6 us (12%)
  local copies, waits for them, and re-layouts  10.3 us (10%)
  starting transfers between devices  3.33 us (3%)
    all_to_all x3, blocking collectives, exchange(): return lax.all_to_all(value, 'dp', split_axis=0, concat_axis=0, tiled=True)  36.8 us
    all_gather x1, waiting for transfers between devices, local(): lax.all_gather(weight, 'dp', axis=0, tiled=True, axis_index_groups=[ring])  12.1 us
    all_to_all x1, waiting for transfers between devices, exchange(): return lax.all_to_all(value, 'dp', split_axis=0, concat_axis=0, tiled=True)  10.8 us
    pallas_call x1, Pallas kernels, local(): pl.pallas_call(functools.partial(product_kernel, order), out_shape=jax.Sh...  8.48 us
    unnamed x19, local copies, waits for them, and re-layouts  3.85 us
    all_to_all x1, starting transfers between devices, exchange(): return lax.all_to_all(value, 'dp', split_axis=0, concat_axis=0, tiled=True)  3.29 us
  transfers between devices with their start and end apart: 2, of which 2 were waited for; matrix products, arithmetic and copies ran while one was open for 7% of the time, Pallas kernels for 4%

profile of v4, /device:TPU:0, one launch (start us, length us, event | category | flops | bytes accessed | tf_op | source)
XLA Modules:
  0.0 103.1 jit_solution(16813986309657130438)
XLA Ops:
  7.2 0.7 all-gather.2.cloned.1.call-update
  7.9 1.1 %reshape.42 = bf16[16,32,32]{2,1,0:T(8,128)(2,1)S(1)} reshape(bf16[16,1024]{1,0:T(8,128)(2,1)} %param.12) | data formatting | bytes 65536 | tf_op jit(solution)/shard_map/reshape | solution.py:138
  9.9 14.5 %all_to_all.20 = bf16[32,5,128]{2,1,0:T(8,128)(2,1)S(1)} all-to-all(bf16[32,5,128]{2,1,0:T(8,128)(2,1)S(1)} %concatenate.11), channel_id=1, replica_groups=mesh['groups'=1,'dp'=32] {'dp'}, dimensions={0} | all-to-all | bytes 81920 | tf_op jit(solution)/shard_map/all_to_all | solution.py:120
  24.8 0.9 copy-done.3
  25.7 0.7 copy-done.6
  26.4 0.9 shard_map.103
  27.3 1.0 reshape.45
  28.3 3.3 %all-to-all-start.1 = ((bf16[32,24,128]{2,1,0:T(8,128)(2,1)}), bf16[32,24,128]{2,1,0:T(8,128)(2,1)}, u32[]{:S(2)}, u32[]{:S(2)}) async-start(bf16[32,24,128]{2,1,0:T(8,128)(2,1)} %reshape.45), calls=%async_computation.1 | async-start | bytes 393216 | tf_op jit(solution)/shard_map/all_to_all | solution.py:120
  32.3 10.8 %all-to-all-done.1 = bf16[32,24,128]{2,1,0:T(8,128)(2,1)} async-done(((bf16[32,24,128]{2,1,0:T(8,128)(2,1)}), bf16[32,24,128]{2,1,0:T(8,128)(2,1)}, u32[]{:S(2)}, u32[]{:S(2)}) %all-to-all-start.1) | async-done | bytes 196640 | tf_op jit(solution)/shard_map/all_to_all | solution.py:120
  43.1 1.1 %reshape.46.got_ref = bf16[32,16,192]{2,1,0:T(8,128)(2,1)S(1)} reshape(bf16[32,24,128]{2,1,0:T(8,128)(2,1)} %all-to-all-done.1) | data formatting | bytes 393216 | tf_op jit(solution)/shard_map/reshape | solution.py:153
  44.2 1.7 %shard_map.104 = (bf16[16,5120]{1,0:T(8,128)(2,1)S(1)}, bf16[16,256]{1,0:T(8,128)(2,1)S(1)}, bf16[32,16,192]{2,1,0:T(8,128)(2,1)S(1)}) custom-call(s32[1]{0:T(128)S(6)} %copy.23.length_ref, bf16[256,5120]{1,0:T(8,128)(2,1)S(1)} %copy-done, bf16[256,1024]{1,0:T(8,128)(2,1)S(1)} %copy-done.1, bf16[32,16,192]{2,1,0:T(8,128)(2,1)S(1)} %reshape.46.got_ref), custom_call_target="tpu_custom_call" | custom-call | tf_op jit(solution)/shard_map/pallas_call | solution.py:155
  45.9 0.7 copy-done.2
  46.6 0.7 copy-done.4
  47.3 0.6 copy-done.5
  47.9 1.3 %reshape.47 = bf16[32,24,128]{2,1,0:T(8,128)(2,1)S(1)} reshape(bf16[32,16,192]{2,1,0:T(8,128)(2,1)} %copy-done.2) | data formatting | bytes 393216 | tf_op jit(solution)/shard_map/reshape | solution.py:167
  49.2 12.9 %all_to_all.21 = bf16[32,24,128]{2,1,0:T(8,128)(2,1)S(1)} all-to-all(bf16[32,24,128]{2,1,0:T(8,128)(2,1)S(1)} %reshape.47), channel_id=1, replica_groups=mesh['groups'=1,'dp'=32] {'dp'}, dimensions={0} | all-to-all | bytes 393216 | tf_op jit(solution)/shard_map/all_to_all | solution.py:120
  62.1 0.2 reshape.48.sums_ref
  62.3 1.5 %shard_map.106 = (f32[160,512]{1,0:T(8,128)}, f32[512,32]{1,0:T(8,128)S(1)}) custom-call(bf16[512,128]{1,0:T(8,128)(2,1)S(1)} %pad_maximum_fusion.met_ref, s32[1,32]{1,0:T(1,128)S(1)} %bitcast.13, bf16[512,192]{1,0:T(8,128)(2,1)S(1)} %reshape.48.sums_ref), custom_call_target="tpu_custom_call" | custom-call | tf_op jit(solution)/shard_map/pallas_call | solution.py:169
  63.9 9.4 %all_to_all.22 = f32[32,1,512]{2,1,0:T(1,128)S(1)} all-to-all(f32[32,1,512]{2,1,0:T(1,128)S(1)} %reshape.51), channel_id=1, replica_groups=mesh['groups'=1,'dp'=32] {'dp'}, dimensions={0} | all-to-all | bytes 131072 | tf_op jit(solution)/shard_map/all_to_all | solution.py:120
  73.3 0.5 broadcast.3
  73.8 0.8 reduce
  74.8 0.8 reshape.50
  75.6 12.1 %all-gather.2.cloned.1.call-done.w_ref = bf16[5120,1024]{1,0:T(8,128)(2,1)} async-done(((bf16[160,1024]{1,0:T(8,128)(2,1)}), bf16[5120,1024]{1,0:T(8,128)(2,1)}) %all-gather.2.cloned.1.call-update) | async-done | bytes 10485776 | tf_op jit(solution)/shard_map/all_gather | solution.py:136
  87.8 8.5 %shard_map.105 = bf16[256,5120]{1,0:T(8,128)(2,1)} custom-call(s32[1]{0:T(128)S(6)} %copy.23.length_ref, bf16[256,1024]{1,0:T(8,128)(2,1)} %dv_ref.3, bf16[16,256]{1,0:T(8,128)(2,1)} %copy-done.5, bf16[16,5120]{1,0:T(8,128)(2,1)} %copy-done.4, bf16[5120,1024]{1,0:T(8,128)(2,1)} %all-gather.2.cloned.1.call-done.w_ref), custom_call_target="tpu_custom_call" | custom-call | tf_op jit(solution)/shard_map/pallas_call | solution.py:187
  (24 shorter events, 0.9 us)
Async XLA Ops:
  7.2 37.0 %copy-start = (bf16[256,5120]{1,0:T(8,128)(2,1)S(1)}, bf16[256,5120]{1,0:T(8,128)(2,1)}, u32[]{:S(2)}) copy-start(bf16[256,5120]{1,0:T(8,128)(2,1)} %x_ref.1) | copy-start | bytes 7864324
  7.2 37.0 %copy-start.1 = (bf16[256,1024]{1,0:T(8,128)(2,1)S(1)}, bf16[256,1024]{1,0:T(8,128)(2,1)}, u32[]{:S(2)}) copy-start(bf16[256,1024]{1,0:T(8,128)(2,1)} %dv_ref.3) | copy-start | bytes 1572868
  7.2 80.6 %all-gather.2.cloned.1.call-start = ((), (), s32[]{:S(2)}) async-start(), calls=%async_computation.4 | async-start | bytes 10813440 | tf_op jit(solution)/shard_map/all_gather | solution.py:136
  24.7 0.9 copy-start.3
  25.7 0.7 copy-start.6
  28.3 14.8 %all-to-all-start.1 = ((bf16[32,24,128]{2,1,0:T(8,128)(2,1)}), bf16[32,24,128]{2,1,0:T(8,128)(2,1)}, u32[]{:S(2)}, u32[]{:S(2)}) async-start(bf16[32,24,128]{2,1,0:T(8,128)(2,1)} %reshape.45), calls=%async_computation.1 | async-start | bytes 393216 | tf_op jit(solution)/shard_map/all_to_all | solution.py:120
  31.6 30.6 %copy-start.7 = (s32[32]{0:T(128)S(1)}, s32[32]{0:T(128)}, u32[]{:S(2)}) copy-start(s32[32]{0:T(128)} %param.15) | copy-start | bytes 388
  45.9 0.7 copy-start.2
  46.6 0.7 copy-start.4
  47.3 0.6 copy-start.5
Sparse Core Ops, SparseCore 0:
  9.6 78.0 all-gather.1

commit v5 on v4

--- a/solution.py
+++ b/solution.py
@@ -9,7 +9,7 @@
 
 RANK = 16
 LANES = 128
-COLUMNS = 256
+COLUMNS = 512
 SCALE = 2.0
 BF16 = jnp.bfloat16
 F32 = jnp.float32
@@ -78,35 +78,35 @@
         out_ref[j, :, rows:rows + chunk] = up_sum[:, j * chunk:(j + 1) * chunk]
 
 
-def product_kernel(order, length_ref, dv_ref, g_ref, down_ref, w_ref, out_ref, held_ref, block_ref, sem, out_sem):
-    groups, places = sem.shape
-    rows = held_ref.shape[1] // places
-    copies = [[] for _ in range(groups)]
+def product_kernel(order, length_ref, dv_ref, g_ref, down_ref, w_ref, out_ref, *scratch):
+    held, columns, sem, out_sem = scratch
+    rows = held.shape[0] // len(order)
+    copies = [None] * len(order)
     for position, block in enumerate(order):
         source = w_ref.at[pl.ds(position * rows, rows)]
-        group, place = block // places, block % places
-        copies[group].append(pltpu.make_async_copy(source, held_ref.at[group, pl.ds(place * rows, rows)], sem.at[group, place]))
-
-    def leave(group):
-        target = out_ref.at[:, pl.ds(group * places * rows, places * rows)]
-        return pltpu.make_async_copy(block_ref.at[group], target, out_sem.at[group])
-
-    for group in copies:
-        for copy in group:
-            copy.start()
+        copies[block] = pltpu.make_async_copy(source, held.at[pl.ds(block * rows, rows)], sem.at[block])
+    for copy in copies:
+        copy.start()
     dv = masked(dv_ref[...], length_ref[0])
     g = g_ref[...]
+    groups = out_sem.shape[0]
+    leaving = []
+    done = 0
     for group in range(groups):
-        for copy in copies[group]:
+        here = len(order) * (group + 1) // groups
+        for copy in copies[len(order) * group // groups:here]:
             copy.wait()
-        for first in range(0, places * rows, COLUMNS):
-            columns = slice(group * places * rows + first, group * places * rows + first + COLUMNS)
-            total = dot(dv, held_ref[group, first:first + COLUMNS], CONTRACT_LANES)
-            total += dot(g, down_ref[:, columns], CONTRACT_ROWS)
-            block_ref[group, :, first:first + COLUMNS] = total.astype(BF16)
-        leave(group).start()
-    for group in range(groups):
-        leave(group).wait()
+        ready = here * rows // COLUMNS * COLUMNS
+        for first in range(done, ready, COLUMNS):
+            part = slice(first, first + COLUMNS)
+            total = dot(dv, held[part], CONTRACT_LANES) + dot(g, down_ref[:, part], CONTRACT_ROWS)
+            columns[:, part] = total.astype(BF16)
+        part = pl.ds(done, ready - done)
+        leaving.append(pltpu.make_async_copy(columns.at[:, part], out_ref.at[:, part], out_sem.at[group]))
+        leaving[-1].start()
+        done = ready
+    for copy in leaving:
+        copy.wait()
 
 
 def snake(sizes):
@@ -183,16 +183,15 @@
     groups = 4
     if block % 16 or chips % groups:
         order, block = list(range(groups)), width // groups
-    places = len(order) // groups
     grad_x = pl.pallas_call(
         functools.partial(product_kernel, order),
         out_shape=jax.ShapeDtypeStruct((tokens, width), BF16),
         in_specs=[SMEM, VMEM, VMEM, VMEM, HBM],
         out_specs=HBM,
         scratch_shapes=[
-            pltpu.VMEM((groups, places * block, value), BF16),
-            pltpu.VMEM((groups, tokens, places * block), BF16),
-            pltpu.SemaphoreType.DMA((groups, places)),
+            pltpu.VMEM((width, value), BF16),
+            pltpu.VMEM((tokens, width), BF16),
+            pltpu.SemaphoreType.DMA((len(order),)),
             pltpu.SemaphoreType.DMA((groups,)),
         ],
         compiler_params=params(60),

time: 103 us -> 103 us (level)
  no operation moved by 1% of the time
where the time goes in v5:
time: 103 us; the launch traced here: 102 us
  blocking collectives  36.8 us (36%)
  waiting for transfers between devices  23.6 us (23%)
  between operations  15.6 us (15%)
  Pallas kernels  11.9 us (12%)
  local copies, waits for them, and re-layouts  10.3 us (10%)
  starting transfers between devices  3.33 us (3%)
    all_to_all x3, blocking collectives, exchange(): return lax.all_to_all(value, 'dp', split_axis=0, concat_axis=0, tiled=True)  36.8 us
    all_gather x1, waiting for transfers between devices, local(): lax.all_gather(weight, 'dp', axis=0, tiled=True, axis_index_groups=[ring])  12.1 us
    all_to_all x1, waiting for transfers between devices, exchange(): return lax.all_to_all(value, 'dp', split_axis=0, concat_axis=0, tiled=True)  10.8 us
    pallas_call x1, Pallas kernels, local(): pl.pallas_call(functools.partial(product_kernel, order), out_shape=jax.Sh...  7.82 us
    unnamed x19, local copies, waits for them, and re-layouts  3.85 us
    all_to_all x1, starting transfers between devices, exchange(): return lax.all_to_all(value, 'dp', split_axis=0, concat_axis=0, tiled=True)  3.29 us
  transfers between devices with their start and end apart: 2, of which 2 were waited for; matrix products, arithmetic and copies ran while one was open for 7% of the time, Pallas kernels for 4%

profile of v5, /device:TPU:0, one launch (start us, length us, event | category | flops | bytes accessed | tf_op | source)
XLA Modules:
  0.0 102.4 jit_solution(13236425620062267994)
XLA Ops:
  7.2 0.7 all-gather.2.cloned.1.call-update
  7.9 1.1 %reshape.42 = bf16[16,32,32]{2,1,0:T(8,128)(2,1)S(1)} reshape(bf16[16,1024]{1,0:T(8,128)(2,1)} %param.12) | data formatting | bytes 65536 | tf_op jit(solution)/shard_map/reshape | solution.py:138
  9.9 14.5 %all_to_all.20 = bf16[32,5,128]{2,1,0:T(8,128)(2,1)S(1)} all-to-all(bf16[32,5,128]{2,1,0:T(8,128)(2,1)S(1)} %concatenate.11), channel_id=1, replica_groups=mesh['groups'=1,'dp'=32] {'dp'}, dimensions={0} | all-to-all | bytes 81920 | tf_op jit(solution)/shard_map/all_to_all | solution.py:120
  24.8 0.9 copy-done.3
  25.7 0.7 copy-done.6
  26.4 0.9 shard_map.103
  27.3 1.0 reshape.45
  28.3 3.3 %all-to-all-start.1 = ((bf16[32,24,128]{2,1,0:T(8,128)(2,1)}), bf16[32,24,128]{2,1,0:T(8,128)(2,1)}, u32[]{:S(2)}, u32[]{:S(2)}) async-start(bf16[32,24,128]{2,1,0:T(8,128)(2,1)} %reshape.45), calls=%async_computation.1 | async-start | bytes 393216 | tf_op jit(solution)/shard_map/all_to_all | solution.py:120
  32.3 10.8 %all-to-all-done.1 = bf16[32,24,128]{2,1,0:T(8,128)(2,1)} async-done(((bf16[32,24,128]{2,1,0:T(8,128)(2,1)}), bf16[32,24,128]{2,1,0:T(8,128)(2,1)}, u32[]{:S(2)}, u32[]{:S(2)}) %all-to-all-start.1) | async-done | bytes 196640 | tf_op jit(solution)/shard_map/all_to_all | solution.py:120
  43.1 1.1 %reshape.46.got_ref = bf16[32,16,192]{2,1,0:T(8,128)(2,1)S(1)} reshape(bf16[32,24,128]{2,1,0:T(8,128)(2,1)} %all-to-all-done.1) | data formatting | bytes 393216 | tf_op jit(solution)/shard_map/reshape | solution.py:153
  44.2 1.7 %shard_map.104 = (bf16[16,5120]{1,0:T(8,128)(2,1)S(1)}, bf16[16,256]{1,0:T(8,128)(2,1)S(1)}, bf16[32,16,192]{2,1,0:T(8,128)(2,1)S(1)}) custom-call(s32[1]{0:T(128)S(6)} %copy.23.length_ref, bf16[256,5120]{1,0:T(8,128)(2,1)S(1)} %copy-done, bf16[256,1024]{1,0:T(8,128)(2,1)S(1)} %copy-done.1, bf16[32,16,192]{2,1,0:T(8,128)(2,1)S(1)} %reshape.46.got_ref), custom_call_target="tpu_custom_call" | custom-call | tf_op jit(solution)/shard_map/pallas_call | solution.py:155
  45.9 0.7 copy-done.2
  46.6 0.7 copy-done.4
  47.3 0.6 copy-done.5
  47.9 1.3 %reshape.47 = bf16[32,24,128]{2,1,0:T(8,128)(2,1)S(1)} reshape(bf16[32,16,192]{2,1,0:T(8,128)(2,1)} %copy-done.2) | data formatting | bytes 393216 | tf_op jit(solution)/shard_map/reshape | solution.py:167
  49.2 12.9 %all_to_all.21 = bf16[32,24,128]{2,1,0:T(8,128)(2,1)S(1)} all-to-all(bf16[32,24,128]{2,1,0:T(8,128)(2,1)S(1)} %reshape.47), channel_id=1, replica_groups=mesh['groups'=1,'dp'=32] {'dp'}, dimensions={0} | all-to-all | bytes 393216 | tf_op jit(solution)/shard_map/all_to_all | solution.py:120
  62.1 0.2 reshape.48.sums_ref
  62.3 1.5 %shard_map.106 = (f32[160,512]{1,0:T(8,128)}, f32[512,32]{1,0:T(8,128)S(1)}) custom-call(bf16[512,128]{1,0:T(8,128)(2,1)S(1)} %pad_maximum_fusion.met_ref, s32[1,32]{1,0:T(1,128)S(1)} %bitcast.13, bf16[512,192]{1,0:T(8,128)(2,1)S(1)} %reshape.48.sums_ref), custom_call_target="tpu_custom_call" | custom-call | tf_op jit(solution)/shard_map/pallas_call | solution.py:169
  63.9 9.4 %all_to_all.22 = f32[32,1,512]{2,1,0:T(1,128)S(1)} all-to-all(f32[32,1,512]{2,1,0:T(1,128)S(1)} %reshape.51), channel_id=1, replica_groups=mesh['groups'=1,'dp'=32] {'dp'}, dimensions={0} | all-to-all | bytes 131072 | tf_op jit(solution)/shard_map/all_to_all | solution.py:120
  73.3 0.5 broadcast.3
  73.8 0.8 reduce
  74.8 0.8 reshape.50
  75.6 12.1 %all-gather.2.cloned.1.call-done.w_ref = bf16[5120,1024]{1,0:T(8,128)(2,1)} async-done(((bf16[160,1024]{1,0:T(8,128)(2,1)}), bf16[5120,1024]{1,0:T(8,128)(2,1)}) %all-gather.2.cloned.1.call-update) | async-done | bytes 10485776 | tf_op jit(solution)/shard_map/all_gather | solution.py:136
  87.8 7.8 %shard_map.105 = bf16[256,5120]{1,0:T(8,128)(2,1)} custom-call(s32[1]{0:T(128)S(6)} %copy.23.length_ref, bf16[256,1024]{1,0:T(8,128)(2,1)} %dv_ref.3, bf16[16,256]{1,0:T(8,128)(2,1)} %copy-done.5, bf16[16,5120]{1,0:T(8,128)(2,1)} %copy-done.4, bf16[5120,1024]{1,0:T(8,128)(2,1)} %all-gather.2.cloned.1.call-done.w_ref), custom_call_target="tpu_custom_call" | custom-call | tf_op jit(solution)/shard_map/pallas_call | solution.py:186
  (24 shorter events, 0.9 us)
Async XLA Ops:
  7.2 37.0 %copy-start = (bf16[256,5120]{1,0:T(8,128)(2,1)S(1)}, bf16[256,5120]{1,0:T(8,128)(2,1)}, u32[]{:S(2)}) copy-start(bf16[256,5120]{1,0:T(8,128)(2,1)} %x_ref.1) | copy-start | bytes 7864324
  7.2 37.0 %copy-start.1 = (bf16[256,1024]{1,0:T(8,128)(2,1)S(1)}, bf16[256,1024]{1,0:T(8,128)(2,1)}, u32[]{:S(2)}) copy-start(bf16[256,1024]{1,0:T(8,128)(2,1)} %dv_ref.3) | copy-start | bytes 1572868
  7.2 80.6 %all-gather.2.cloned.1.call-start = ((), (), s32[]{:S(2)}) async-start(), calls=%async_computation.4 | async-start | bytes 10813440 | tf_op jit(solution)/shard_map/all_gather | solution.py:136
  24.7 0.9 copy-start.3
  25.7 0.7 copy-start.6
  28.3 14.8 %all-to-all-start.1 = ((bf16[32,24,128]{2,1,0:T(8,128)(2,1)}), bf16[32,24,128]{2,1,0:T(8,128)(2,1)}, u32[]{:S(2)}, u32[]{:S(2)}) async-start(bf16[32,24,128]{2,1,0:T(8,128)(2,1)} %reshape.45), calls=%async_computation.1 | async-start | bytes 393216 | tf_op jit(solution)/shard_map/all_to_all | solution.py:120
  31.6 30.6 %copy-start.7 = (s32[32]{0:T(128)S(1)}, s32[32]{0:T(128)}, u32[]{:S(2)}) copy-start(s32[32]{0:T(128)} %param.15) | copy-start | bytes 388
  45.9 0.7 copy-start.2
  46.6 0.7 copy-start.4
  47.3 0.6 copy-start.5
Sparse Core Ops, SparseCore 0:
  9.6 78.0 all-gather.1

commit v6 on v5

--- a/solution.py
+++ b/solution.py
@@ -79,7 +79,7 @@
 
 
 def product_kernel(order, length_ref, dv_ref, g_ref, down_ref, w_ref, out_ref, *scratch):
-    held, columns, sem, out_sem = scratch
+    held, columns, adapter, sem, out_sem = scratch
     rows = held.shape[0] // len(order)
     copies = [None] * len(order)
     for position, block in enumerate(order):
@@ -89,6 +89,9 @@
         copy.start()
     dv = masked(dv_ref[...], length_ref[0])
     g = g_ref[...]
+    for first in range(0, held.shape[0], COLUMNS):
+        part = slice(first, first + COLUMNS)
+        adapter[:, part] = dot(g, down_ref[:, part], CONTRACT_ROWS)
     groups = out_sem.shape[0]
     leaving = []
     done = 0
@@ -99,8 +102,7 @@
         ready = here * rows // COLUMNS * COLUMNS
         for first in range(done, ready, COLUMNS):
             part = slice(first, first + COLUMNS)
-            total = dot(dv, held[part], CONTRACT_LANES) + dot(g, down_ref[:, part], CONTRACT_ROWS)
-            columns[:, part] = total.astype(BF16)
+            columns[:, part] = (dot(dv, held[part], CONTRACT_LANES) + adapter[:, part]).astype(BF16)
         part = pl.ds(done, ready - done)
         leaving.append(pltpu.make_async_copy(columns.at[:, part], out_ref.at[:, part], out_sem.at[group]))
         leaving[-1].start()
@@ -191,6 +193,7 @@
         scratch_shapes=[
             pltpu.VMEM((width, value), BF16),
             pltpu.VMEM((tokens, width), BF16),
+            pltpu.VMEM((tokens, width), F32),
             pltpu.SemaphoreType.DMA((len(order),)),
             pltpu.SemaphoreType.DMA((groups,)),
         ],

time: 103 us -> 102 us (level)
  no operation moved by 1% of the time
where the time goes in v6:
time: 102 us
  blocking collectives  36.8 us (36%)
  waiting for transfers between devices  23.6 us (23%)
  between operations  15.6 us (15%)
  Pallas kernels  11.5 us (11%)
  local copies, waits for them, and re-layouts  10.3 us (10%)
  starting transfers between devices  3.33 us (3%)
    all_to_all x3, blocking collectives, exchange(): return lax.all_to_all(value, 'dp', split_axis=0, concat_axis=0, tiled=True)  36.8 us
    all_gather x1, waiting for transfers between devices, local(): lax.all_gather(weight, 'dp', axis=0, tiled=True, axis_index_groups=[ring])  12.1 us
    all_to_all x1, waiting for transfers between devices, exchange(): return lax.all_to_all(value, 'dp', split_axis=0, concat_axis=0, tiled=True)  10.8 us
    pallas_call x1, Pallas kernels, local(): pl.pallas_call(functools.partial(product_kernel, order), out_shape=jax.Sh...  7.41 us
    unnamed x19, local copies, waits for them, and re-layouts  3.85 us
    all_to_all x1, starting transfers between devices, exchange(): return lax.all_to_all(value, 'dp', split_axis=0, concat_axis=0, tiled=True)  3.29 us
  transfers between devices with their start and end apart: 2, of which 2 were waited for; matrix products, arithmetic and copies ran while one was open for 7% of the time, Pallas kernels for 4%

profile of v6, /device:TPU:0, one launch (start us, length us, event | category | flops | bytes accessed | tf_op | source)
XLA Modules:
  0.0 102.0 jit_solution(16408710473526365337)
XLA Ops:
  7.2 0.7 all-gather.2.cloned.1.call-update
  7.9 1.1 %reshape.42 = bf16[16,32,32]{2,1,0:T(8,128)(2,1)S(1)} reshape(bf16[16,1024]{1,0:T(8,128)(2,1)} %param.12) | data formatting | bytes 65536 | tf_op jit(solution)/shard_map/reshape | solution.py:140
  9.9 14.5 %all_to_all.20 = bf16[32,5,128]{2,1,0:T(8,128)(2,1)S(1)} all-to-all(bf16[32,5,128]{2,1,0:T(8,128)(2,1)S(1)} %concatenate.11), channel_id=1, replica_groups=mesh['groups'=1,'dp'=32] {'dp'}, dimensions={0} | all-to-all | bytes 81920 | tf_op jit(solution)/shard_map/all_to_all | solution.py:122
  24.8 0.9 copy-done.3
  25.7 0.7 copy-done.6
  26.4 0.9 shard_map.103
  27.3 1.0 reshape.45
  28.3 3.3 %all-to-all-start.1 = ((bf16[32,24,128]{2,1,0:T(8,128)(2,1)}), bf16[32,24,128]{2,1,0:T(8,128)(2,1)}, u32[]{:S(2)}, u32[]{:S(2)}) async-start(bf16[32,24,128]{2,1,0:T(8,128)(2,1)} %reshape.45), calls=%async_computation.1 | async-start | bytes 393216 | tf_op jit(solution)/shard_map/all_to_all | solution.py:122
  32.3 10.8 %all-to-all-done.1 = bf16[32,24,128]{2,1,0:T(8,128)(2,1)} async-done(((bf16[32,24,128]{2,1,0:T(8,128)(2,1)}), bf16[32,24,128]{2,1,0:T(8,128)(2,1)}, u32[]{:S(2)}, u32[]{:S(2)}) %all-to-all-start.1) | async-done | bytes 196640 | tf_op jit(solution)/shard_map/all_to_all | solution.py:122
  43.1 1.1 %reshape.46.got_ref = bf16[32,16,192]{2,1,0:T(8,128)(2,1)S(1)} reshape(bf16[32,24,128]{2,1,0:T(8,128)(2,1)} %all-to-all-done.1) | data formatting | bytes 393216 | tf_op jit(solution)/shard_map/reshape | solution.py:155
  44.2 1.7 %shard_map.104 = (bf16[16,5120]{1,0:T(8,128)(2,1)S(1)}, bf16[16,256]{1,0:T(8,128)(2,1)S(1)}, bf16[32,16,192]{2,1,0:T(8,128)(2,1)S(1)}) custom-call(s32[1]{0:T(128)S(6)} %copy.23.length_ref, bf16[256,5120]{1,0:T(8,128)(2,1)S(1)} %copy-done, bf16[256,1024]{1,0:T(8,128)(2,1)S(1)} %copy-done.1, bf16[32,16,192]{2,1,0:T(8,128)(2,1)S(1)} %reshape.46.got_ref), custom_call_target="tpu_custom_call" | custom-call | tf_op jit(solution)/shard_map/pallas_call | solution.py:157
  45.9 0.7 copy-done.2
  46.6 0.7 copy-done.4
  47.3 0.6 copy-done.5
  47.9 1.3 %reshape.47 = bf16[32,24,128]{2,1,0:T(8,128)(2,1)S(1)} reshape(bf16[32,16,192]{2,1,0:T(8,128)(2,1)} %copy-done.2) | data formatting | bytes 393216 | tf_op jit(solution)/shard_map/reshape | solution.py:169
  49.2 12.9 %all_to_all.21 = bf16[32,24,128]{2,1,0:T(8,128)(2,1)S(1)} all-to-all(bf16[32,24,128]{2,1,0:T(8,128)(2,1)S(1)} %reshape.47), channel_id=1, replica_groups=mesh['groups'=1,'dp'=32] {'dp'}, dimensions={0} | all-to-all | bytes 393216 | tf_op jit(solution)/shard_map/all_to_all | solution.py:122
  62.1 0.2 reshape.48.sums_ref
  62.3 1.5 %shard_map.106 = (f32[160,512]{1,0:T(8,128)}, f32[512,32]{1,0:T(8,128)S(1)}) custom-call(bf16[512,128]{1,0:T(8,128)(2,1)S(1)} %pad_maximum_fusion.met_ref, s32[1,32]{1,0:T(1,128)S(1)} %bitcast.13, bf16[512,192]{1,0:T(8,128)(2,1)S(1)} %reshape.48.sums_ref), custom_call_target="tpu_custom_call" | custom-call | tf_op jit(solution)/shard_map/pallas_call | solution.py:171
  63.9 9.4 %all_to_all.22 = f32[32,1,512]{2,1,0:T(1,128)S(1)} all-to-all(f32[32,1,512]{2,1,0:T(1,128)S(1)} %reshape.51), channel_id=1, replica_groups=mesh['groups'=1,'dp'=32] {'dp'}, dimensions={0} | all-to-all | bytes 131072 | tf_op jit(solution)/shard_map/all_to_all | solution.py:122
  73.3 0.5 broadcast.3
  73.8 0.8 reduce
  74.8 0.8 reshape.50
  75.6 12.1 %all-gather.2.cloned.1.call-done.w_ref = bf16[5120,1024]{1,0:T(8,128)(2,1)} async-done(((bf16[160,1024]{1,0:T(8,128)(2,1)}), bf16[5120,1024]{1,0:T(8,128)(2,1)}) %all-gather.2.cloned.1.call-update) | async-done | bytes 10485776 | tf_op jit(solution)/shard_map/all_gather | solution.py:138
  87.8 7.4 %shard_map.105 = bf16[256,5120]{1,0:T(8,128)(2,1)} custom-call(s32[1]{0:T(128)S(6)} %copy.23.length_ref, bf16[256,1024]{1,0:T(8,128)(2,1)} %dv_ref.3, bf16[16,256]{1,0:T(8,128)(2,1)} %copy-done.5, bf16[16,5120]{1,0:T(8,128)(2,1)} %copy-done.4, bf16[5120,1024]{1,0:T(8,128)(2,1)} %all-gather.2.cloned.1.call-done.w_ref), custom_call_target="tpu_custom_call" | custom-call | tf_op jit(solution)/shard_map/pallas_call | solution.py:188
  (24 shorter events, 0.9 us)
Async XLA Ops:
  7.2 37.0 %copy-start = (bf16[256,5120]{1,0:T(8,128)(2,1)S(1)}, bf16[256,5120]{1,0:T(8,128)(2,1)}, u32[]{:S(2)}) copy-start(bf16[256,5120]{1,0:T(8,128)(2,1)} %x_ref.1) | copy-start | bytes 7864324
  7.2 37.0 %copy-start.1 = (bf16[256,1024]{1,0:T(8,128)(2,1)S(1)}, bf16[256,1024]{1,0:T(8,128)(2,1)}, u32[]{:S(2)}) copy-start(bf16[256,1024]{1,0:T(8,128)(2,1)} %dv_ref.3) | copy-start | bytes 1572868
  7.2 80.6 %all-gather.2.cloned.1.call-start = ((), (), s32[]{:S(2)}) async-start(), calls=%async_computation.4 | async-start | bytes 10813440 | tf_op jit(solution)/shard_map/all_gather | solution.py:138
  24.7 0.9 copy-start.3
  25.7 0.7 copy-start.6
  28.3 14.8 %all-to-all-start.1 = ((bf16[32,24,128]{2,1,0:T(8,128)(2,1)}), bf16[32,24,128]{2,1,0:T(8,128)(2,1)}, u32[]{:S(2)}, u32[]{:S(2)}) async-start(bf16[32,24,128]{2,1,0:T(8,128)(2,1)} %reshape.45), calls=%async_computation.1 | async-start | bytes 393216 | tf_op jit(solution)/shard_map/all_to_all | solution.py:122
  31.6 30.6 %copy-start.7 = (s32[32]{0:T(128)S(1)}, s32[32]{0:T(128)}, u32[]{:S(2)}) copy-start(s32[32]{0:T(128)} %param.15) | copy-start | bytes 388
  45.9 0.7 copy-start.2
  46.6 0.7 copy-start.4
  47.3 0.6 copy-start.5
Sparse Core Ops, SparseCore 0:
  9.6 78.0 all-gather.1
